TPU v7x, 128 devices: a whole 4x4x4 slice. The times are simulated.
128 devices in a mesh: axial: 8 (over y, z_hi), azim: 16 (over z_lo, x, core).
Axes of the slice: x: 4, y: 4, z: 4 (z_hi: 2, z_lo: 2; z = z_hi * 2 + z_lo), core: 2. Of those that a mesh axis runs over, the one named last changes fastest.
Arguments:
- gas: float32 [13, 64, 512, 128], P(None, 'axial', 'azim'), may hold values from -6 to 6
- diffusivity: float32 [13], replicated, may hold values from 0.04 to 0.12
- swirl: float32 [64, 512, 128], P('axial', 'azim'), may hold values from 0.1 to 0.25
- drops: float32 [2048, 13, 128], P(('axial', 'azim')), may hold values from -6 to 6
- mass: float32 [2048, 128], P(('axial', 'azim')), may hold values from 0.2 to 5
- azim_weight: float32 [2048, 128], P(('axial', 'azim')), may hold values from 0 to 1
- cell_index: int32 [2048, 128], P(('axial', 'azim')), may hold values from 0 to 32767, as said below
- bin_rows: int32 [2048], P(('axial', 'azim')), may hold values from 0 to 128, as said below
- destination: int32 [2048, 1], P(('axial', 'azim')), may hold values from 0 to 15; in each aligned block of 16 rows (0 to 15, 16 to 31, ...) at most 2 rows name the same one
Outputs:
- gas_out: float32 [13, 64, 512, 128], P(None, 'axial', 'azim')
- moved_drops: float32 [4096, 13, 128], P(('axial', 'azim'))
- moved_rows: int32 [4096], P(('axial', 'azim'))
Inputs may be any that keep to these rules, and one draw needn't show every extreme that they name: `bin_rows`: each bin holds 0 to 128 live rows, and some bin holds 128. `destination`: among the 16 bins of one device no sector is named more than 2 times. `cell_index`: some droplet lies in its block's first cell and some in its last.
All inputs are finite; a program needn't handle non-finite values.
Results may differ from a plain program's by a relative error of at most 0.0003.
Values sent between devices are 32-bit elements; how exact they have to be, the bound alone decides.
A program may use at most 192 MiB of HBM per device.

v0:
```python
import jax
import jax.numpy as jnp
from jax import lax
from jax.sharding import PartitionSpec as P

SUBSTEPS = 4
CAP = 2


source_load = 2.0


def extended(shard, sides, width, wrap):
    for axis, dim in sides:
        size, length = (lax.axis_size(axis), shard.shape[dim])
        up = [(i, (i + 1) % size) for i in range(size if wrap else size - 1)]
        down = [(j, i) for i, j in up]
        last = lax.slice_in_dim(shard, length - width, length, axis=dim)
        initial = lax.slice_in_dim(shard, 0, width, axis=dim)
        before = lax.ppermute(last, axis, up)
        after = lax.ppermute(initial, axis, down)
        shard = jnp.concatenate([before, shard, after], axis=dim)
    return shard


def from_behind(shard, axis, by):
    size = lax.axis_size(axis)
    return lax.ppermute(shard, axis, [(i, (i + by) % size) for i in range(size)])


def body(gas, diffusivity, swirl, drops, mass, azim_weight, cell_index, bin_rows, destination):
    nvar, cells_a, cells_t, cells_r = gas.shape
    nbins = drops.shape[0]
    brows = drops.shape[2]
    sectors = lax.axis_size("azim")
    rows = jnp.arange(brows, dtype=jnp.int32)
    live = (rows[None, :] < bin_rows[:, None]).astype(jnp.float32)
    a_loc = cell_index // (cells_t * cells_r)
    t_loc = cell_index // cells_r % cells_t
    r_loc = cell_index % cells_r
    first = (a_loc * (cells_t + 2) + t_loc + 1) * cells_r + r_loc
    second = first + cells_r
    near = 1.0 - azim_weight
    near_wide = near[None]
    upper_wide = azim_weight[None]
    diff = diffusivity[:, None, None, None]
    carried = jnp.swapaxes(drops, 0, 1)
    for step in range(SUBSTEPS):
        sector_padded = extended(gas, (("azim", 2),), 1, True)
        slab_partitioned_field = extended(gas, (("axial", 1),), 1, False)
        field = sector_padded.reshape(nvar, -1)
        lower = jnp.take(field, first, axis=1)
        upper = jnp.take(field, second, axis=1)
        sample = near_wide * lower + upper_wide * upper
        rate = 0.5 * mass / (1.0 + mass) * (1.0 + 0.5 * jnp.tanh(sample[0])) * live
        transfer = rate[None] * (carried - sample)
        carried = carried - transfer
        part_low = source_load * near_wide * transfer
        part_high = source_load * upper_wide * transfer
        deposit = jnp.zeros_like(field).at[:, first].add(part_low).at[:, second].add(part_high)
        deposit = deposit.reshape(sector_padded.shape)
        incoming = from_behind(deposit[:, :, cells_t + 1 :, :], "azim", 1)
        inner = deposit[:, :, 1 : cells_t + 1, :]
        source = inner + jnp.pad(incoming, ((0, 0), (0, 0), (0, cells_t - 1), (0, 0)))
        radial = jnp.pad(gas, ((0, 0), (0, 0), (0, 0), (1, 1)))
        behind = sector_padded[:, :, :-2, :]
        adjacent_neighbour_cells = behind + sector_padded[:, :, 2:, :]
        adjacent_neighbour_cells = (
            adjacent_neighbour_cells
            + slab_partitioned_field[:, 2:, :, :]
            + slab_partitioned_field[:, :-2, :, :]
        )
        adjacent_neighbour_cells = (
            adjacent_neighbour_cells + radial[:, :, :, 2:] + radial[:, :, :, :-2]
        )
        gas = (
            gas
            + diff * (adjacent_neighbour_cells - 6.0 * gas)
            - swirl[None] * (gas - behind)
            + source
        )
    payload = jnp.swapaxes(carried * live[None], 0, 1)
    target = destination[:, 0]
    row_count = bin_rows.astype(jnp.float32)
    every, complete_bin_rows, every_target = (
        lax.all_gather(payload, "azim", axis=0, tiled=True),
        lax.all_gather(row_count, "azim", axis=0, tiled=True),
        lax.all_gather(target.astype(jnp.float32), "azim", axis=0, tiled=True),
    )
    goal = every_target.astype(jnp.int32)
    total = goal.shape[0]
    order = jnp.arange(total, dtype=jnp.int32)
    anchor = order // nbins
    previous_gas_state = (
        (goal[:, None] == goal[None, :])
        & (anchor[:, None] == anchor[None, :])
        & (order[None, :] < order[:, None])
    )
    rank = jnp.sum(previous_gas_state.astype(jnp.int32), axis=1)
    mine = goal == lax.axis_index("azim")
    slot = jnp.where(mine, anchor * CAP + rank, sectors * CAP)
    moved_drops = (
        jnp.zeros((sectors * CAP, nvar, brows), jnp.float32).at[slot].set(every, mode="drop")
    )
    moved_rows = (
        jnp.zeros((sectors * CAP,), jnp.float32)
        .at[slot]
        .set(complete_bin_rows, mode="drop")
        .astype(jnp.int32)
    )
    return (gas, moved_drops, moved_rows)


def solution(mesh):
    return jax.shard_map(
        body,
        mesh=mesh,
        in_specs=(
            P(None, "axial", "azim", None),
            P(),
            P("axial", "azim", None),
            P(("axial", "azim"), None, None),
            P(("axial", "azim"), None),
            P(("axial", "azim"), None),
            P(("axial", "azim"), None),
            P(("axial", "azim")),
            P(("axial", "azim"), None),
        ),
        out_specs=(
            P(None, "axial", "azim", None),
            P(("axial", "azim"), None, None),
            P(("axial", "azim")),
        ),
        check_vma=False,
    )
```

profile of v0, /device:TPU:0, one launch (start us, length us, event | category | flops | bytes accessed | tf_op | source)
XLA Modules:
  0.0 560.7 jit_solution(7239413253040188118)
XLA Ops:
  8.5 3.8 collective-permute-start.1
  12.4 1.8 fusion.106
  15.5 7.2 %collective-permute-start.3 = (f32[13,1,32,128]{3,2,1,0:T(8,128)}, f32[13,1,32,128]{3,2,1,0:T(8,128)}, u32[]{:S(2)}, u32[]{:S(2)}) collective-permute-start(f32[13,1,32,128]{3,2,1,0:T(8,128)} %get-tuple-element.35), channel_id=1, source_target_pairs={{0,16},{16,32},{32,48},{48,64},{64,80},{80,96},{96,112},{1,17},{17... | collective-permute-start | bytes 638984 | tf_op jit(solution)/shard_map/ppermute | solution.py:20
  25.4 1.8 pad_maximum_fusion
  27.2 9.1 %copy.70 = f32[13,8,34,128]{0,3,2,1:T(8,128)} copy(f32[13,8,34,128]{3,2,1,0:T(8,128)S(1)} %pad_maximum_fusion) | data formatting | bytes 3620864 | tf_op jit(solution)/shard_map/concatenate | solution.py:22
  36.3 11.5 %gather_fusion = f32[2048,13]{1,0:T(8,128)S(1)} fusion(f32[13,34816]{0,1:T(8,128)} %bitcast.136, s32[2048]{0:T(1024)S(1)} %get-tuple-element.45), kind=kCustom, calls=%fused_computation.clone | custom fusion | bytes 221184 | tf_op jit(solution)/shard_map/jit(_take)/gather | solution.py:52
  48.2 11.5 %gather_fusion.1 = f32[2048,13]{1,0:T(8,128)S(1)} fusion(f32[13,34816]{0,1:T(8,128)} %bitcast.137, s32[2048]{0:T(1024)S(1)} %get-tuple-element.46), kind=kCustom, calls=%fused_computation.1.clone | custom fusion | bytes 221184 | tf_op jit(solution)/shard_map/jit(_take)/gather | solution.py:53
  61.6 18.7 %scatter_custom_fusion = f32[13,34816]{0,1:T(8,128)} fusion(s32[2048]{0:T(1024)S(1)} %fusion.94, f32[2048,13]{1,0:T(8,128)S(1)} %bitcast.157, f32[]{:T(128)} %constant.92.clone.1), kind=kCustom, calls=%fused_computation.24 | custom fusion | flops 26624 | bytes 1810436 | tf_op jit(solution)/shard_map/scatter-add | solution.py:60
  80.3 22.5 %scatter_fusion = f32[13,34816]{0,1:T(8,128)} fusion(f32[13,34816]{0,1:T(8,128)} %scatter_custom_fusion, s32[2048]{0:T(1024)S(1)} %get-tuple-element.18, f32[2048,13]{1,0:T(8,128)S(1)} %bitcast.145), kind=kCustom, calls=%fused_computation.9 | custom fusion | flops 26624 | bytes 327680 | tf_op jit(solution)/shard_map/scatter-add | solution.py:60
  104.7 11.7 %slice.241 = f32[13,8,32,128]{0,3,2,1:T(8,128)} slice(f32[13,8,34,128]{0,3,2,1:T(8,128)} %bitcast.131), slice={[0:13], [0:8], [1:33], [0:128]} | slice | bytes 3407872 | tf_op jit(solution)/shard_map/slice | solution.py:63
  116.4 11.1 %copy.108 = f32[13,8,32,128]{3,2,1,0:T(8,128)} copy(f32[13,8,32,128]{0,3,2,1:T(8,128)} %slice.241) | data formatting | bytes 3407872
  128.1 3.3 fusion.14
  131.6 3.9 collective-permute-start.6
  137.6 7.0 %collective-permute-start.8 = (f32[13,1,32,128]{3,2,1,0:T(8,128)}, f32[13,1,32,128]{3,2,1,0:T(8,128)}, u32[]{:S(2)}, u32[]{:S(2)}) collective-permute-start(f32[13,1,32,128]{3,2,1,0:T(8,128)} %get-tuple-element.31), channel_id=1, source_target_pairs={{0,16},{16,32},{32,48},{48,64},{64,80},{80,96},{96,112},{1,17},{17... | collective-permute-start | bytes 638984 | tf_op jit(solution)/shard_map/ppermute | solution.py:20
  144.6 1.7 pad_maximum_fusion.1
  146.3 10.3 %copy.77 = f32[13,8,34,128]{0,3,2,1:T(8,128)} copy(f32[13,8,34,128]{3,2,1,0:T(8,128)} %pad_maximum_fusion.1) | data formatting | bytes 3620864 | tf_op jit(solution)/shard_map/concatenate | solution.py:22
  156.6 13.7 %gather_fusion.2 = f32[2048,13]{1,0:T(8,128)} fusion(f32[13,34816]{0,1:T(8,128)} %bitcast.140, s32[2048]{0:T(1024)S(1)} %copy-done.23), kind=kCustom, calls=%fused_computation.2.clone | custom fusion | bytes 221184 | tf_op jit(solution)/shard_map/jit(_take)/gather | solution.py:52
  170.4 11.6 %gather_fusion.3 = f32[2048,13]{1,0:T(8,128)S(1)} fusion(f32[13,34816]{0,1:T(8,128)} %bitcast.141, s32[2048]{0:T(1024)S(1)} %get-tuple-element.46), kind=kCustom, calls=%fused_computation.3.clone | custom fusion | bytes 221184 | tf_op jit(solution)/shard_map/jit(_take)/gather | solution.py:53
  185.9 19.1 %scatter_custom_fusion.2 = f32[13,34816]{0,1:T(8,128)} fusion(s32[2048]{0:T(1024)} %copy-done.67, f32[2048,13]{1,0:T(8,128)} %bitcast.158, f32[]{:T(128)} %constant.92.clone.1), kind=kCustom, calls=%fused_computation.22 | custom fusion | flops 26624 | bytes 1810944 | tf_op jit(solution)/shard_map/scatter-add | solution.py:60
  205.0 22.5 %scatter_fusion.1 = f32[13,34816]{0,1:T(8,128)} fusion(f32[13,34816]{0,1:T(8,128)} %scatter_custom_fusion.2, s32[2048]{0:T(1024)S(1)} %get-tuple-element.18, f32[2048,13]{1,0:T(8,128)S(1)} %bitcast.146), kind=kCustom, calls=%fused_computation.11 | custom fusion | flops 26624 | bytes 327680 | tf_op jit(solution)/shard_map/scatter-add | solution.py:60
  229.0 11.7 %slice.248 = f32[13,8,32,128]{0,3,2,1:T(8,128)} slice(f32[13,8,34,128]{0,3,2,1:T(8,128)} %bitcast.133), slice={[0:13], [0:8], [1:33], [0:128]} | slice | bytes 3407872 | tf_op jit(solution)/shard_map/slice | solution.py:63
  240.7 11.0 %copy.110 = f32[13,8,32,128]{3,2,1,0:T(8,128)} copy(f32[13,8,32,128]{0,3,2,1:T(8,128)} %slice.248) | data formatting | bytes 3407872
  252.3 3.3 fusion.21
  255.8 3.9 collective-permute-start.11
  261.8 7.0 %collective-permute-start.13 = (f32[13,1,32,128]{3,2,1,0:T(8,128)}, f32[13,1,32,128]{3,2,1,0:T(8,128)}, u32[]{:S(2)}, u32[]{:S(2)}) collective-permute-start(f32[13,1,32,128]{3,2,1,0:T(8,128)} %get-tuple-element.27), channel_id=1, source_target_pairs={{0,16},{16,32},{32,48},{48,64},{64,80},{80,96},{96,112},{1,17},{17... | collective-permute-start | bytes 638984 | tf_op jit(solution)/shard_map/ppermute | solution.py:20
  270.0 1.7 pad_maximum_fusion.2
  271.8 10.3 %copy.84 = f32[13,8,34,128]{0,3,2,1:T(8,128)} copy(f32[13,8,34,128]{3,2,1,0:T(8,128)} %pad_maximum_fusion.2) | data formatting | bytes 3620864 | tf_op jit(solution)/shard_map/concatenate | solution.py:22
  282.1 13.7 %gather_fusion.4 = f32[2048,13]{1,0:T(8,128)} fusion(f32[13,34816]{0,1:T(8,128)} %bitcast.142, s32[2048]{0:T(1024)S(1)} %copy-done.24), kind=kCustom, calls=%fused_computation.4.clone | custom fusion | bytes 221184 | tf_op jit(solution)/shard_map/jit(_take)/gather | solution.py:52
  295.9 11.6 %gather_fusion.5 = f32[2048,13]{1,0:T(8,128)S(1)} fusion(f32[13,34816]{0,1:T(8,128)} %bitcast.143, s32[2048]{0:T(1024)S(1)} %get-tuple-element.46), kind=kCustom, calls=%fused_computation.5.clone | custom fusion | bytes 221184 | tf_op jit(solution)/shard_map/jit(_take)/gather | solution.py:53
  311.5 19.1 %scatter_custom_fusion.4 = f32[13,34816]{0,1:T(8,128)} fusion(s32[2048]{0:T(1024)} %copy-done.67, f32[2048,13]{1,0:T(8,128)} %bitcast.159, f32[]{:T(128)} %constant.92.clone.1), kind=kCustom, calls=%fused_computation.20 | custom fusion | flops 26624 | bytes 1810944 | tf_op jit(solution)/shard_map/scatter-add | solution.py:60
  330.6 22.5 %scatter_fusion.2 = f32[13,34816]{0,1:T(8,128)} fusion(f32[13,34816]{0,1:T(8,128)} %scatter_custom_fusion.4, s32[2048]{0:T(1024)S(1)} %get-tuple-element.18, f32[2048,13]{1,0:T(8,128)S(1)} %bitcast.147), kind=kCustom, calls=%fused_computation.13 | custom fusion | flops 26624 | bytes 327680 | tf_op jit(solution)/shard_map/scatter-add | solution.py:60
  354.6 11.7 %slice.255 = f32[13,8,32,128]{0,3,2,1:T(8,128)} slice(f32[13,8,34,128]{0,3,2,1:T(8,128)} %bitcast.135), slice={[0:13], [0:8], [1:33], [0:128]} | slice | bytes 3407872 | tf_op jit(solution)/shard_map/slice | solution.py:63
  366.3 11.0 %copy.112 = f32[13,8,32,128]{3,2,1,0:T(8,128)} copy(f32[13,8,32,128]{0,3,2,1:T(8,128)} %slice.255) | data formatting | bytes 3407872
  377.9 3.3 fusion.28
  381.4 3.9 collective-permute-start.16
  387.1 1.7 pad_maximum_fusion.3
  388.8 10.3 %copy.91 = f32[13,8,34,128]{0,3,2,1:T(8,128)} copy(f32[13,8,34,128]{3,2,1,0:T(8,128)} %pad_maximum_fusion.3) | data formatting | bytes 3620864 | tf_op jit(solution)/shard_map/concatenate | solution.py:22
  399.2 11.5 %gather_fusion.6 = f32[2048,13]{1,0:T(8,128)S(1)} fusion(f32[13,34816]{0,1:T(8,128)} %bitcast.138, s32[2048]{0:T(1024)S(1)} %copy-done.25), kind=kCustom, calls=%fused_computation.6.clone | custom fusion | bytes 221184 | tf_op jit(solution)/shard_map/jit(_take)/gather | solution.py:52
  410.8 13.7 %gather_fusion.7 = f32[2048,13]{1,0:T(8,128)} fusion(f32[13,34816]{0,1:T(8,128)} %bitcast.139, s32[2048]{0:T(1024)S(1)} %get-tuple-element.46), kind=kCustom, calls=%fused_computation.7.clone | custom fusion | bytes 221184 | tf_op jit(solution)/shard_map/jit(_take)/gather | solution.py:53
  428.8 31.1 %all-reduce.10 = (f32[256]{0:T(256)S(1)}, f32[256]{0:T(256)S(1)}) all-reduce(f32[256]{0:T(256)S(1)} %bitcast_dynamic-update-slice_fusion, f32[256]{0:T(256)S(1)} %convert_dynamic-update-slice_fusion), channel_id=2, replica_groups=mesh['axial'=8,'azim'=16] {'azim'}, use_global_device_ids=true, to_apply=%add.8 | all-reduce | flops 512 | bytes 4096
  462.3 7.1 %collective-permute-start.18 = (f32[13,1,32,128]{3,2,1,0:T(8,128)}, f32[13,1,32,128]{3,2,1,0:T(8,128)}, u32[]{:S(2)}, u32[]{:S(2)}) collective-permute-start(f32[13,1,32,128]{3,2,1,0:T(8,128)} %get-tuple-element.23), channel_id=1, source_target_pairs={{0,16},{16,32},{32,48},{48,64},{64,80},{80,96},{96,112},{1,17},{17... | collective-permute-start | bytes 638984 | tf_op jit(solution)/shard_map/ppermute | solution.py:20
  471.1 19.1 %scatter_custom_fusion.6 = f32[13,34816]{0,1:T(8,128)} fusion(s32[2048]{0:T(1024)} %copy-done.67, f32[2048,13]{1,0:T(8,128)} %bitcast.156, f32[]{:T(128)} %constant.92.clone.1), kind=kCustom, calls=%fused_computation.18 | custom fusion | flops 26624 | bytes 1810944 | tf_op jit(solution)/shard_map/scatter-add | solution.py:60
  490.2 22.5 %scatter_fusion.3 = f32[13,34816]{0,1:T(8,128)} fusion(f32[13,34816]{0,1:T(8,128)} %scatter_custom_fusion.6, s32[2048]{0:T(1024)S(1)} %get-tuple-element.18, f32[2048,13]{1,0:T(8,128)S(1)} %bitcast.144), kind=kCustom, calls=%fused_computation.15 | custom fusion | flops 26624 | bytes 327680 | tf_op jit(solution)/shard_map/scatter-add | solution.py:60
  516.8 11.7 %slice.262 = f32[13,8,32,128]{0,3,2,1:T(8,128)} slice(f32[13,8,34,128]{0,3,2,1:T(8,128)} %bitcast.129), slice={[0:13], [0:8], [1:33], [0:128]} | slice | bytes 3407872 | tf_op jit(solution)/shard_map/slice | solution.py:63
  528.4 10.1 %copy.114 = f32[13,8,32,128]{3,2,1,0:T(8,128)S(1)} copy(f32[13,8,32,128]{0,3,2,1:T(8,128)} %slice.262) | data formatting | bytes 3407872
  538.6 4.0 fusion.35
  542.6 2.5 copy.98
  545.1 7.6 %scatter_fusion.4 = f32[32,13,128]{2,1,0:T(8,128)S(1)} fusion(f32[32,13,128]{2,1,0:T(8,128)S(1)} %broadcast_in_dim.24, s32[256]{0:T(256)S(1)} %compare_select_fusion.3, f32[256,13,128]{2,1,0:T(8,128)S(1)} %copy.98), kind=kCustom, calls=%fused_computation.16 | custom fusion | bytes 5112832 | tf_op jit(solution)/shard_map/scatter | solution.py:103
  (242 shorter events, 41.8 us)
Async XLA Ops:
  7.2 535.4 %all-gather.3.cloned.1.call-start = ((), (), s32[]{:S(2)}) async-start(), calls=%async_computation | async-start | bytes 1810432 | tf_op jit(solution)/shard_map/all_gather | solution.py:86
  8.4 15.8 %collective-permute-start = (f32[13,8,1,128]{3,2,1,0:T(1,128)S(1)}, f32[13,8,1,128]{3,2,1,0:T(1,128)S(1)}, u32[]{:S(2)}, u32[]{:S(2)}) collective-permute-start(f32[13,8,1,128]{3,2,1,0:T(1,128)S(1)} %get-tuple-element.32), channel_id=1, source_target_pairs={{0,1},{1,2},{2,3},{3,4},{4,5},{5,6},{6,7},{7,8},{8,9},{9,10},{10,1... | collective-permute-start | bytes 159752 | tf_op jit(solution)/shard_map/ppermute | solution.py:20
  8.5 15.7 %collective-permute-start.1 = (f32[13,8,1,128]{3,2,1,0:T(1,128)S(1)}, f32[13,8,1,128]{3,2,1,0:T(1,128)S(1)}, u32[]{:S(2)}, u32[]{:S(2)}) collective-permute-start(f32[13,8,1,128]{3,2,1,0:T(1,128)S(1)} %get-tuple-element.33), channel_id=1, source_target_pairs={{1,0},{2,1},{3,2},{4,3},{5,4},{6,5},{7,6},{8,7},{9,8},{10,9},{11,1... | collective-permute-start | bytes 159752 | tf_op jit(solution)/shard_map/ppermute | solution.py:21
  14.2 113.3 %collective-permute-start.2 = (f32[13,1,32,128]{3,2,1,0:T(8,128)}, f32[13,1,32,128]{3,2,1,0:T(8,128)}, u32[]{:S(2)}, u32[]{:S(2)}) collective-permute-start(f32[13,1,32,128]{3,2,1,0:T(8,128)} %get-tuple-element.34), channel_id=1, source_target_pairs={{16,0},{32,16},{48,32},{64,48},{80,64},{96,80},{112,96},{17,1},{33... | collective-permute-start | bytes 638984 | tf_op jit(solution)/shard_map/ppermute | solution.py:21
  15.5 112.6 %collective-permute-start.3 = (f32[13,1,32,128]{3,2,1,0:T(8,128)}, f32[13,1,32,128]{3,2,1,0:T(8,128)}, u32[]{:S(2)}, u32[]{:S(2)}) collective-permute-start(f32[13,1,32,128]{3,2,1,0:T(8,128)} %get-tuple-element.35), channel_id=1, source_target_pairs={{0,16},{16,32},{32,48},{48,64},{64,80},{80,96},{96,112},{1,17},{17... | collective-permute-start | bytes 638984 | tf_op jit(solution)/shard_map/ppermute | solution.py:20
  23.4 38.2 %copy-start.67 = (s32[2048]{0:T(1024)}, s32[2048]{0:T(1024)S(1)}, u32[]{:S(2)}) copy-start(s32[2048]{0:T(1024)S(1)} %fusion.94) | copy-start | bytes 24580
  24.2 36.0 %copy-start.34 = (f32[16,128]{1,0:T(8,128)}, f32[16,128]{1,0:T(8,128)S(1)}, u32[]{:S(2)}) copy-start(f32[16,128]{1,0:T(8,128)S(1)} %get-tuple-element.42) | copy-start | bytes 24580
  24.2 36.1 %copy-start.30 = (f32[16,128]{1,0:T(8,128)}, f32[16,128]{1,0:T(8,128)S(1)}, u32[]{:S(2)}) copy-start(f32[16,128]{1,0:T(8,128)S(1)} %get-tuple-element.40) | copy-start | bytes 24580
  24.2 36.1 %copy-start.38 = (f32[16,128]{1,0:T(8,128)}, f32[16,128]{1,0:T(8,128)S(1)}, u32[]{:S(2)}) copy-start(f32[16,128]{1,0:T(8,128)S(1)} %get-tuple-element.41) | copy-start | bytes 24580
  24.2 35.9 %copy-start.54 = (pred[16,128]{1,0:T(8,128)(4,1)}, pred[16,128]{1,0:T(8,128)(4,1)S(1)}, u32[]{:S(2)}) copy-start(pred[16,128]{1,0:T(8,128)(4,1)S(1)} %get-tuple-element.43) | copy-start | bytes 6148
  24.2 35.9 %copy-start.58 = (pred[16,128]{1,0:T(8,128)(4,1)}, pred[16,128]{1,0:T(8,128)(4,1)S(1)}, u32[]{:S(2)}) copy-start(pred[16,128]{1,0:T(8,128)(4,1)S(1)} %get-tuple-element.44) | copy-start | bytes 6148
  104.1 23.3 %collective-permute-start.4 = (f32[13,8,1,128]{3,2,1,0:T(1,128)S(1)}, f32[13,8,1,128]{3,2,1,0:T(1,128)S(1)}, u32[]{:S(2)}, u32[]{:S(2)}) collective-permute-start(f32[13,8,1,128]{3,2,1,0:T(1,128)S(1)} %copy.109), channel_id=1, source_target_pairs={{0,1},{1,2},{2,3},{3,4},{4,5},{5,6},{6,7},{7,8},{8,9},{9,10},{10,1... | collective-permute-start | bytes 159752 | tf_op jit(solution)/shard_map/ppermute | solution.py:28
  131.5 13.0 %collective-permute-start.5 = (f32[13,8,1,128]{3,2,1,0:T(1,128)S(1)}, f32[13,8,1,128]{3,2,1,0:T(1,128)S(1)}, u32[]{:S(2)}, u32[]{:S(2)}) collective-permute-start(f32[13,8,1,128]{3,2,1,0:T(1,128)S(1)} %get-tuple-element.28), channel_id=1, source_target_pairs={{0,1},{1,2},{2,3},{3,4},{4,5},{5,6},{6,7},{7,8},{8,9},{9,10},{10,1... | collective-permute-start | bytes 159752 | tf_op jit(solution)/shard_map/ppermute | solution.py:20
  131.6 13.0 %collective-permute-start.6 = (f32[13,8,1,128]{3,2,1,0:T(1,128)S(1)}, f32[13,8,1,128]{3,2,1,0:T(1,128)S(1)}, u32[]{:S(2)}, u32[]{:S(2)}) collective-permute-start(f32[13,8,1,128]{3,2,1,0:T(1,128)S(1)} %get-tuple-element.29), channel_id=1, source_target_pairs={{1,0},{2,1},{3,2},{4,3},{5,4},{6,5},{7,6},{8,7},{9,8},{10,9},{11,1... | collective-permute-start | bytes 159752 | tf_op jit(solution)/shard_map/ppermute | solution.py:21
  136.3 115.4 %collective-permute-start.7 = (f32[13,1,32,128]{3,2,1,0:T(8,128)}, f32[13,1,32,128]{3,2,1,0:T(8,128)}, u32[]{:S(2)}, u32[]{:S(2)}) collective-permute-start(f32[13,1,32,128]{3,2,1,0:T(8,128)} %get-tuple-element.30), channel_id=1, source_target_pairs={{16,0},{32,16},{48,32},{64,48},{80,64},{96,80},{112,96},{17,1},{33... | collective-permute-start | bytes 638984 | tf_op jit(solution)/shard_map/ppermute | solution.py:21
  137.6 114.7 %collective-permute-start.8 = (f32[13,1,32,128]{3,2,1,0:T(8,128)}, f32[13,1,32,128]{3,2,1,0:T(8,128)}, u32[]{:S(2)}, u32[]{:S(2)}) collective-permute-start(f32[13,1,32,128]{3,2,1,0:T(8,128)} %get-tuple-element.31), channel_id=1, source_target_pairs={{0,16},{16,32},{32,48},{48,64},{64,80},{80,96},{96,112},{1,17},{17... | collective-permute-start | bytes 638984 | tf_op jit(solution)/shard_map/ppermute | solution.py:20
  170.4 13.8 %copy-start.3 = (f32[13,16,128]{2,1,0:T(8,128)S(1)}, f32[13,16,128]{2,1,0:T(8,128)}, u32[]{:S(2)}) copy-start(f32[13,16,128]{2,1,0:T(8,128)} %copy-done.2) | copy-start | bytes 319492
  184.2 20.8 %copy-start.10 = (f32[13,16,128]{2,1,0:T(8,128)}, f32[13,16,128]{2,1,0:T(8,128)S(1)}, u32[]{:S(2)}) copy-start(f32[13,16,128]{2,1,0:T(8,128)S(1)} %get-tuple-element.17) | copy-start | bytes 319492
  228.8 22.9 %collective-permute-start.9 = (f32[13,8,1,128]{3,2,1,0:T(1,128)S(1)}, f32[13,8,1,128]{3,2,1,0:T(1,128)S(1)}, u32[]{:S(2)}, u32[]{:S(2)}) collective-permute-start(f32[13,8,1,128]{3,2,1,0:T(1,128)S(1)} %copy.111), channel_id=1, source_target_pairs={{0,1},{1,2},{2,3},{3,4},{4,5},{5,6},{6,7},{7,8},{8,9},{9,10},{10,1... | collective-permute-start | bytes 159752 | tf_op jit(solution)/shard_map/ppermute | solution.py:28
  255.7 13.1 %collective-permute-start.10 = (f32[13,8,1,128]{3,2,1,0:T(1,128)S(1)}, f32[13,8,1,128]{3,2,1,0:T(1,128)S(1)}, u32[]{:S(2)}, u32[]{:S(2)}) collective-permute-start(f32[13,8,1,128]{3,2,1,0:T(1,128)S(1)} %get-tuple-element.24), channel_id=1, source_target_pairs={{0,1},{1,2},{2,3},{3,4},{4,5},{5,6},{6,7},{7,8},{8,9},{9,10},{10,1... | collective-permute-start | bytes 159752 | tf_op jit(solution)/shard_map/ppermute | solution.py:20
  255.8 13.0 %collective-permute-start.11 = (f32[13,8,1,128]{3,2,1,0:T(1,128)S(1)}, f32[13,8,1,128]{3,2,1,0:T(1,128)S(1)}, u32[]{:S(2)}, u32[]{:S(2)}) collective-permute-start(f32[13,8,1,128]{3,2,1,0:T(1,128)S(1)} %get-tuple-element.25), channel_id=1, source_target_pairs={{1,0},{2,1},{3,2},{4,3},{5,4},{6,5},{7,6},{8,7},{9,8},{10,9},{11,1... | collective-permute-start | bytes 159752 | tf_op jit(solution)/shard_map/ppermute | solution.py:21
  260.5 116.8 %collective-permute-start.12 = (f32[13,1,32,128]{3,2,1,0:T(8,128)}, f32[13,1,32,128]{3,2,1,0:T(8,128)}, u32[]{:S(2)}, u32[]{:S(2)}) collective-permute-start(f32[13,1,32,128]{3,2,1,0:T(8,128)} %get-tuple-element.26), channel_id=1, source_target_pairs={{16,0},{32,16},{48,32},{64,48},{80,64},{96,80},{112,96},{17,1},{33... | collective-permute-start | bytes 638984 | tf_op jit(solution)/shard_map/ppermute | solution.py:21
  261.8 116.1 %collective-permute-start.13 = (f32[13,1,32,128]{3,2,1,0:T(8,128)}, f32[13,1,32,128]{3,2,1,0:T(8,128)}, u32[]{:S(2)}, u32[]{:S(2)}) collective-permute-start(f32[13,1,32,128]{3,2,1,0:T(8,128)} %get-tuple-element.27), channel_id=1, source_target_pairs={{0,16},{16,32},{32,48},{48,64},{64,80},{80,96},{96,112},{1,17},{17... | collective-permute-start | bytes 638984 | tf_op jit(solution)/shard_map/ppermute | solution.py:20
  295.8 13.8 %copy-start.4 = (f32[13,16,128]{2,1,0:T(8,128)S(1)}, f32[13,16,128]{2,1,0:T(8,128)}, u32[]{:S(2)}) copy-start(f32[13,16,128]{2,1,0:T(8,128)} %copy-done.2) | copy-start | bytes 319492
  295.9 13.8 %copy-start.9 = (f32[16,13,128]{2,0,1:T(8,128)S(1)}, f32[16,13,128]{2,0,1:T(8,128)}, u32[]{:S(2)}) copy-start(f32[16,13,128]{2,0,1:T(8,128)} %param.14) | copy-start | bytes 319492
  295.9 13.8 %copy-start.11 = (f32[13,16,128]{2,1,0:T(8,128)S(1)}, f32[13,16,128]{2,1,0:T(8,128)}, u32[]{:S(2)}) copy-start(f32[13,16,128]{2,1,0:T(8,128)} %copy-done.10) | copy-start | bytes 319492
  295.9 13.8 %copy-start.32 = (f32[16,128]{1,0:T(8,128)S(1)}, f32[16,128]{1,0:T(8,128)}, u32[]{:S(2)}) copy-start(f32[16,128]{1,0:T(8,128)} %copy-done.30) | copy-start | bytes 24580
  295.9 13.8 %copy-start.44 = (f32[16,128]{1,0:T(8,128)S(1)}, f32[16,128]{1,0:T(8,128)}, u32[]{:S(2)}) copy-start(f32[16,128]{1,0:T(8,128)} %copy-done.42) | copy-start | bytes 24580
  309.6 21.0 %copy-start.5 = (f32[13,16,128]{2,1,0:T(8,128)}, f32[13,16,128]{2,1,0:T(8,128)S(1)}, u32[]{:S(2)}) copy-start(f32[13,16,128]{2,1,0:T(8,128)S(1)} %fusion.58) | copy-start | bytes 319492
  309.7 20.9 %copy-start.49 = (f32[16,128]{1,0:T(8,128)}, f32[16,128]{1,0:T(8,128)S(1)}, u32[]{:S(2)}) copy-start(f32[16,128]{1,0:T(8,128)S(1)} %fusion.80) | copy-start | bytes 24580
  309.7 20.8 %copy-start.12 = (f32[13,16,128]{2,1,0:T(8,128)}, f32[13,16,128]{2,1,0:T(8,128)S(1)}, u32[]{:S(2)}) copy-start(f32[13,16,128]{2,1,0:T(8,128)S(1)} %get-tuple-element.15) | copy-start | bytes 319492
  354.4 22.9 %collective-permute-start.14 = (f32[13,8,1,128]{3,2,1,0:T(1,128)S(1)}, f32[13,8,1,128]{3,2,1,0:T(1,128)S(1)}, u32[]{:S(2)}, u32[]{:S(2)}) collective-permute-start(f32[13,8,1,128]{3,2,1,0:T(1,128)S(1)} %copy.113), channel_id=1, source_target_pairs={{0,1},{1,2},{2,3},{3,4},{4,5},{5,6},{6,7},{7,8},{8,9},{9,10},{10,1... | collective-permute-start | bytes 159752 | tf_op jit(solution)/shard_map/ppermute | solution.py:28
  381.3 5.7 %collective-permute-start.15 = (f32[13,8,1,128]{3,2,1,0:T(1,128)S(1)}, f32[13,8,1,128]{3,2,1,0:T(1,128)S(1)}, u32[]{:S(2)}, u32[]{:S(2)}) collective-permute-start(f32[13,8,1,128]{3,2,1,0:T(1,128)S(1)} %get-tuple-element.20), channel_id=1, source_target_pairs={{0,1},{1,2},{2,3},{3,4},{4,5},{5,6},{6,7},{7,8},{8,9},{9,10},{10,1... | collective-permute-start | bytes 159752 | tf_op jit(solution)/shard_map/ppermute | solution.py:20
  381.4 5.7 %collective-permute-start.16 = (f32[13,8,1,128]{3,2,1,0:T(1,128)S(1)}, f32[13,8,1,128]{3,2,1,0:T(1,128)S(1)}, u32[]{:S(2)}, u32[]{:S(2)}) collective-permute-start(f32[13,8,1,128]{3,2,1,0:T(1,128)S(1)} %get-tuple-element.21), channel_id=1, source_target_pairs={{1,0},{2,1},{3,2},{4,3},{5,4},{6,5},{7,6},{8,7},{9,8},{10,9},{11,1... | collective-permute-start | bytes 159752 | tf_op jit(solution)/shard_map/ppermute | solution.py:21
  410.7 15.8 %copy-start.29 = (f32[16,128]{1,0:T(8,128)S(1)}, f32[16,128]{1,0:T(8,128)}, u32[]{:S(2)}) copy-start(f32[16,128]{1,0:T(8,128)} %param.16) | copy-start | bytes 24580
  410.7 15.8 %copy-start.37 = (f32[16,128]{1,0:T(8,128)S(1)}, f32[16,128]{1,0:T(8,128)}, u32[]{:S(2)}) copy-start(f32[16,128]{1,0:T(8,128)} %copy-done.34) | copy-start | bytes 24580
  410.7 15.8 %copy-start.57 = (pred[16,128]{1,0:T(8,128)(4,1)S(1)}, pred[16,128]{1,0:T(8,128)(4,1)}, u32[]{:S(2)}) copy-start(pred[16,128]{1,0:T(8,128)(4,1)} %copy-done.54) | copy-start | bytes 6148
  410.7 15.8 %copy-start.61 = (pred[16,128]{1,0:T(8,128)(4,1)S(1)}, pred[16,128]{1,0:T(8,128)(4,1)}, u32[]{:S(2)}) copy-start(pred[16,128]{1,0:T(8,128)(4,1)} %copy-done.58) | copy-start | bytes 6148
  410.7 15.8 %copy-start.48 = (f32[16,128]{1,0:T(8,128)S(1)}, f32[16,128]{1,0:T(8,128)}, u32[]{:S(2)}) copy-start(f32[16,128]{1,0:T(8,128)} %param.15) | copy-start | bytes 24580
  410.8 15.8 %copy-start.66 = (s32[16]{0:T(128)S(1)}, s32[16]{0:T(128)}, u32[]{:S(2)}) copy-start(s32[16]{0:T(128)} %param.18) | copy-start | bytes 196
  410.8 15.9 %copy-start.6 = (f32[13,16,128]{2,1,0:T(8,128)S(1)}, f32[13,16,128]{2,1,0:T(8,128)}, u32[]{:S(2)}) copy-start(f32[13,16,128]{2,1,0:T(8,128)} %copy-done.5) | copy-start | bytes 319492
  410.8 15.9 %copy-start.13 = (f32[13,16,128]{2,1,0:T(8,128)S(1)}, f32[13,16,128]{2,1,0:T(8,128)}, u32[]{:S(2)}) copy-start(f32[13,16,128]{2,1,0:T(8,128)} %copy-done.12) | copy-start | bytes 319492
  410.8 15.9 %copy-start.50 = (f32[16,128]{1,0:T(8,128)S(1)}, f32[16,128]{1,0:T(8,128)}, u32[]{:S(2)}) copy-start(f32[16,128]{1,0:T(8,128)} %copy-done.49) | copy-start | bytes 24580
  424.9 44.5 %copy-start.33 = (f32[16,128]{1,0:T(8,128)S(1)}, f32[16,128]{1,0:T(8,128)}, u32[]{:S(2)}) copy-start(f32[16,128]{1,0:T(8,128)} %copy-done.30) | copy-start | bytes 24580
  424.9 44.5 %copy-start.41 = (f32[16,128]{1,0:T(8,128)S(1)}, f32[16,128]{1,0:T(8,128)}, u32[]{:S(2)}) copy-start(f32[16,128]{1,0:T(8,128)} %copy-done.38) | copy-start | bytes 24580
  461.0 77.5 %collective-permute-start.17 = (f32[13,1,32,128]{3,2,1,0:T(8,128)}, f32[13,1,32,128]{3,2,1,0:T(8,128)}, u32[]{:S(2)}, u32[]{:S(2)}) collective-permute-start(f32[13,1,32,128]{3,2,1,0:T(8,128)} %get-tuple-element.22), channel_id=1, source_target_pairs={{16,0},{32,16},{48,32},{64,48},{80,64},{96,80},{112,96},{17,1},{33... | collective-permute-start | bytes 638984 | tf_op jit(solution)/shard_map/ppermute | solution.py:21
  462.3 76.3 %collective-permute-start.18 = (f32[13,1,32,128]{3,2,1,0:T(8,128)}, f32[13,1,32,128]{3,2,1,0:T(8,128)}, u32[]{:S(2)}, u32[]{:S(2)}) collective-permute-start(f32[13,1,32,128]{3,2,1,0:T(8,128)} %get-tuple-element.23), channel_id=1, source_target_pairs={{0,16},{16,32},{32,48},{48,64},{64,80},{80,96},{96,112},{1,17},{17... | collective-permute-start | bytes 638984 | tf_op jit(solution)/shard_map/ppermute | solution.py:20
  514.6 24.0 %collective-permute-start.19 = (f32[13,8,1,128]{3,2,1,0:T(1,128)}, f32[13,8,1,128]{3,2,1,0:T(1,128)}, u32[]{:S(2)}, u32[]{:S(2)}) collective-permute-start(f32[13,8,1,128]{3,2,1,0:T(1,128)} %copy.115), channel_id=1, source_target_pairs={{0,1},{1,2},{2,3},{3,4},{4,5},{5,6},{6,7},{7,8},{8,9},{9,10},{10,1... | collective-permute-start | bytes 159752 | tf_op jit(solution)/shard_map/ppermute | solution.py:28
  (44 other events, 365.0 us)
Sparse Core Ops, SparseCore 0:
  427.5 36.5 all-gather.2
where the time goes:
time: 572 us; the launch traced here: 561 us
  local copies, waits for them, and re-layouts  270 us (47%)
  other arithmetic  191 us (33%)
  starting transfers between devices  50.5 us (9%)
  blocking collectives  31.1 us (5%)
  between operations  16.3 us (3%)
    scatter-add x8, other arithmetic, body(): jnp.zeros_like(field).at[:, first].add(part_low).at[:, second]  166 us
    gather x8, local copies, waits for them, and re-layouts, body(): lower = jnp.take(field, first, axis=1)  54.2 us
    gather x8, local copies, waits for them, and re-layouts, body(): upper = jnp.take(field, second, axis=1)  51.1 us
    unnamed x154, local copies, waits for them, and re-layouts  50.9 us
    slice x4, local copies, waits for them, and re-layouts, body(): inner = deposit[:, :, 1:cells_t + 1, :]  46.7 us
    concatenate x4, local copies, waits for them, and re-layouts, extended(): shard = jnp.concatenate([before, shard, after], axis=dim)  40.1 us
    unnamed x1, blocking collectives  31.1 us
    ppermute x8, starting transfers between devices, extended(): before = lax.ppermute(last, axis, up)  28.5 us
  transfers between devices with their start and end apart: 21, of which 1 were waited for; matrix products, arithmetic and copies ran while one was open for 70% of the time, Pallas kernels for 0%

commit v1 on v0

v1 whole, which is shorter than its diff:
```python
import functools

import jax
import jax.numpy as jnp
from jax import lax
from jax.experimental import pallas as pl
from jax.experimental.pallas import tpu as pltpu
from jax.sharding import PartitionSpec as P

MESH = pl.DeviceIdType.MESH
F32, BF16 = jnp.float32, jnp.bfloat16

SUBSTEPS = 4
CAP = 2
NV, CA, CT, CR = 13, 8, 32, 128
NBIN, BROWS = 16, 128
DROPLETS = NBIN * BROWS
LANES = CA * CR
MAIN = NV * CT
VROWS = 16
ROWS = 2 * MAIN + 2 * VROWS
CHUNK = 256

ORDER = (1, 2, 3, 4, 5, 6, 0, 7)
PLACE = {a: i for i, a in enumerate(ORDER)}
INNER, OUTER = (0, 768), (768, 256)


def lanes_of(a):
    return pl.ds(PLACE[a] * CR, CR)


def split(x):
    hi = x.astype(BF16)
    return hi, (x - hi.astype(F32)).astype(BF16)


def kernel(
    sectors, slabs,
    gas, diffusivity, swirl, drops, mass, azim_weight, cell_index, bin_rows, destination,
    gas_out, moved_out,
    G, F, R, RT, W, L, D, Q, T, OUT, DEP, AX, LOW, HIGH, DEPR, FIRST, LAST, PAY, GOT,
    load_sem, save_sem, ax_send, ax_recv, low_send, low_recv, high_send, high_recv, dep_send, dep_recv,
    pay_send, pay_recv,
):
    ax, az = lax.axis_index("axial"), lax.axis_index("azim")
    up_az, down_az = lax.rem(az + 1, sectors), lax.rem(az + sectors - 1, sectors)
    up_ax, down_ax = lax.rem(ax + 1, slabs), lax.rem(ax + slabs - 1, slabs)
    has_up, has_down = ax < slabs - 1, ax > 0
    parts = (OUTER, INNER)

    def load(a):
        return pltpu.make_async_copy(gas.at[:, a], G.at[0, :, :, lanes_of(a)], load_sem.at[a])

    def save(a):
        return pltpu.make_async_copy(
            G.at[SUBSTEPS % 2, :, :, lanes_of(a)], gas_out.at[:, a], save_sem.at[a]
        )

    def axial(src_up, src_down, s):
        upward = pltpu.make_async_remote_copy(
            src_up, AX.at[s, 0], ax_send.at[s, 0], ax_recv.at[s, 0],
            device_id=(up_ax, az), device_id_type=MESH,
        )
        downward = pltpu.make_async_remote_copy(
            src_down, AX.at[s, 1], ax_send.at[s, 1], ax_recv.at[s, 1],
            device_id=(down_ax, az), device_id_type=MESH,
        )
        return upward, downward

    def axial_of(s):
        buf = lax.rem(s, 2)
        return axial(G.at[buf, :, :, lanes_of(CA - 1)], G.at[buf, :, :, lanes_of(0)], s)

    def axial_start(copies):
        upward, downward = copies

        @pl.when(has_up)
        def _():
            upward.start()

        @pl.when(has_down)
        def _():
            downward.start()

    def axial_wait_send(copies):
        upward, downward = copies

        @pl.when(has_up)
        def _():
            upward.wait_send()

        @pl.when(has_down)
        def _():
            downward.wait_send()

    def axial_wait_recv(copies):
        upward, downward = copies

        @pl.when(has_down)
        def _():
            upward.wait_recv()

        @pl.when(has_up)
        def _():
            downward.wait_recv()

    def azim_of(s, p):
        lanes = pl.ds(*parts[p])
        low = pltpu.make_async_remote_copy(
            LAST.at[:, lanes], LOW.at[s, :, lanes], low_send.at[s, p], low_recv.at[s, p],
            device_id=(ax, up_az), device_id_type=MESH,
        )
        high = pltpu.make_async_remote_copy(
            FIRST.at[:, lanes], HIGH.at[s, :, lanes], high_send.at[s, p], high_recv.at[s, p],
            device_id=(ax, down_az), device_id_type=MESH,
        )
        return low, high

    def dep_of(s, p):
        lanes = pl.ds(*parts[p])
        return pltpu.make_async_remote_copy(
            DEP.at[pl.ds(MAIN, VROWS), lanes], DEPR.at[s, :, lanes], dep_send.at[s, p], dep_recv.at[s, p],
            device_id=(ax, up_az), device_id_type=MESH,
        )

    def pay_of(j):
        there = lax.rem(az + j, sectors)
        return pltpu.make_async_remote_copy(
            PAY.at[pl.ds(there * CAP, CAP)], GOT.at[pl.ds(az * CAP, CAP)], pay_send.at[j], pay_recv.at[j],
            device_id=(ax, there), device_id_type=MESH,
        )

    for a in (0, 7, 1, 2, 3, 4, 5, 6):
        load(a).start()
    barrier = pltpu.get_barrier_semaphore()
    for j in range(1, sectors):
        pl.semaphore_signal(
            barrier, inc=1, device_id=(ax, lax.rem(az + j, sectors)), device_id_type=MESH
        )
    for other in (up_ax, down_ax):
        pl.semaphore_signal(barrier, inc=1, device_id=(other, az), device_id_type=MESH)
    pl.semaphore_wait(barrier, sectors + 1)
    axial_start(axial(gas.at[:, CA - 1], gas.at[:, 0], 0))

    @pl.when(jnp.logical_not(has_down))
    def _():
        AX[:, 0] = jnp.zeros((SUBSTEPS, NV, CT, CR), F32)

    @pl.when(jnp.logical_not(has_up))
    def _():
        AX[:, 1] = jnp.zeros((SUBSTEPS, NV, CT, CR), F32)

    FIRST[...] = jnp.zeros((VROWS, LANES), F32)
    LAST[...] = jnp.zeros((VROWS, LANES), F32)
    for a in range(CA):
        load(a).wait()
    for v in range(NV):
        FIRST[v : v + 1, :] = G[0, v, 0:1, :]
        LAST[v : v + 1, :] = G[0, v, CT - 1 : CT, :]
    for p in range(2):
        for copy in azim_of(0, p):
            copy.start()

    cell = cell_index[...]
    layer = cell // (CT * CR)
    place = jnp.where(layer == 0, CA - 2, jnp.where(layer == CA - 1, CA - 1, layer - 1))
    key = place * CR + cell % CR
    key_row = jnp.concatenate([key[b : b + 1] for b in range(NBIN)], axis=1)
    cell_row = jnp.concatenate([cell[b : b + 1] for b in range(NBIN)], axis=1)
    weight = jnp.concatenate([azim_weight[b : b + 1, :] for b in range(NBIN)], axis=1)
    m = mass[...]
    lane = lax.broadcasted_iota(jnp.int32, (1, BROWS), 1)
    half = 0.5 * m / (1.0 + m)
    live = [(lane < bin_rows[b]).astype(F32) for b in range(NBIN)]
    Q[0:1, :] = jnp.concatenate([half[b : b + 1] * live[b] for b in range(NBIN)], axis=1)
    Q[1:2, :] = jnp.where(key_row >= OUTER[0], 1.0, 0.0)
    azim_row = cell_row // CR % CT
    for t0 in range(0, 40, 8):
        t = lax.broadcasted_iota(jnp.int32, (8, DROPLETS), 0) + t0
        W[t0 : t0 + 8, :] = jnp.where(t == azim_row, 1.0 - weight, 0.0) + jnp.where(
            t == azim_row + 1, weight, 0.0
        )
    D[...] = jnp.zeros((VROWS, DROPLETS), F32)
    T[...] = jnp.zeros((VROWS, DROPLETS), F32)
    for b in range(NBIN):
        D[0:NV, b * BROWS : (b + 1) * BROWS] = drops[b]
    for k in range(0, LANES, 16):
        rows = lax.broadcasted_iota(jnp.int32, (16, DROPLETS), 0) + k
        R[k : k + 16, :] = jnp.where(rows == key_row, 1.0, 0.0).astype(BF16)
    key_column = jnp.transpose(key.astype(F32)).astype(jnp.int32)
    for b in range(NBIN):
        for k in range(0, LANES, CR):
            columns = lax.broadcasted_iota(jnp.int32, (BROWS, CR), 1) + k
            RT[b * BROWS : (b + 1) * BROWS, k : k + CR] = jnp.where(
                columns == key_column[:, b : b + 1], 1.0, 0.0
            ).astype(BF16)
    for v in range(NV):
        hi, lo = split(G[0, v])
        F[v * CT : (v + 1) * CT, :] = hi
        F[MAIN + v * CT : MAIN + (v + 1) * CT, :] = lo

    def droplets(s, p):
        start, width = parts[p]
        lanes = pl.ds(start, width)
        for copy in azim_of(s, p)[1:]:
            copy.wait_recv()
        hi, lo = split(HIGH[s, :, lanes])
        F[2 * MAIN : 2 * MAIN + VROWS, lanes] = hi
        F[2 * MAIN + VROWS : ROWS, lanes] = lo
        for c in range(0, DROPLETS, CHUNK):
            ps = pl.ds(c, CHUNK)
            x = jnp.dot(F[:, lanes], R[lanes, ps], preferred_element_type=F32)
            near = (x[:MAIN] + x[MAIN : 2 * MAIN]).reshape(NV, CT, CHUNK)
            far = x[2 * MAIN : 2 * MAIN + VROWS] + x[2 * MAIN + VROWS :]
            w, w_far = W[0:CT, ps], W[CT : CT + 1, ps]
            sample = jnp.sum(near * w[None], axis=1) + w_far * far[0:NV]
            rate = Q[0:1, ps] * (1.0 + 0.5 * jnp.tanh(sample[0:1]))
            carried = D[0:NV, ps]
            transfer = rate * (carried - sample)
            if p == 0:
                OUT[0:NV, ps] = transfer
            else:
                D[0:NV, ps] = carried - jnp.where(Q[1:2, ps] > 0.0, OUT[0:NV, ps], transfer)
            T[0:NV, ps] = 2.0 * transfer
            for v in range(NV):
                hi, lo = split(w * T[v : v + 1, ps])
                L[v * CT : (v + 1) * CT, ps] = hi
                L[MAIN + v * CT : MAIN + (v + 1) * CT, ps] = lo
            hi, lo = split(w_far * T[:, ps])
            L[2 * MAIN : 2 * MAIN + VROWS, ps] = hi
            L[2 * MAIN + VROWS : ROWS, ps] = lo

        if p == 0:
            @pl.when(s > 0)
            def _():
                for q in range(2):
                    dep_of(s - 1, q).wait_send()

        for k in range(start, start + width, CHUNK):
            ks = pl.ds(k, CHUNK)
            x = jnp.dot(L[...], RT[:, ks], preferred_element_type=F32)
            DEP[0:MAIN, ks] = x[:MAIN] + x[MAIN : 2 * MAIN]
            DEP[MAIN : MAIN + VROWS, ks] = x[2 * MAIN : 2 * MAIN + VROWS] + x[2 * MAIN + VROWS :]
        dep_of(s, p).start()

    def stencil(s, p):
        now = lax.rem(s, 2)
        later = 1 - now
        azim_of(s, p)[0].wait_recv()
        dep_of(s, p).wait_recv()
        row = lax.broadcasted_iota(jnp.int32, (CT, CR), 0)
        column = lax.broadcasted_iota(jnp.int32, (CT, CR), 1)
        for v in range(NV):
            d = diffusivity[v]
            one = pl.ds(v, 1)
            for a in ((0, CA - 1) if p == 0 else range(1, CA - 1)):
                here = lanes_of(a)
                c = G[now, v, :, here]
                below = AX[s, 0, v] if a == 0 else G[now, v, :, lanes_of(a - 1)]
                above = AX[s, 1, v] if a == CA - 1 else G[now, v, :, lanes_of(a + 1)]
                behind = jnp.where(row == 0, LOW[s, one, here], pltpu.roll(c, 1, 0))
                ahead = jnp.where(row == CT - 1, HIGH[s, one, here], pltpu.roll(c, CT - 1, 0))
                inward = jnp.where(column == 0, 0.0, pltpu.roll(c, 1, 1))
                outward = jnp.where(column == CR - 1, 0.0, pltpu.roll(c, CR - 1, 1))
                around = behind + ahead + above + below + outward + inward
                source = DEP[v * CT : (v + 1) * CT, here]
                source = source + jnp.where(row == 0, DEPR[s, one, here], 0.0)
                new = c + d * (around - 6.0 * c) - swirl[a] * (c - behind) + source
                G[later, v, :, here] = new
                hi, lo = split(new)
                F[v * CT : (v + 1) * CT, here] = hi
                F[MAIN + v * CT : MAIN + (v + 1) * CT, here] = lo
                FIRST[one, here] = new[0:1]
                LAST[one, here] = new[CT - 1 : CT]

    def send_bins():
        slot = []
        for b in range(NBIN):
            rank = jnp.int32(0)
            for e in range(b):
                rank = rank + jnp.where(destination[e, 0] == destination[b, 0], 1, 0)
            slot.append(destination[b, 0] * CAP + rank)
        row = lax.broadcasted_iota(jnp.int32, (VROWS, BROWS), 0)
        pay = [
            jnp.where(
                row == NV, bin_rows[b].astype(F32), D[:, b * BROWS : (b + 1) * BROWS] * live[b]
            )
            for b in range(NBIN)
        ]
        for k in range(sectors * CAP):
            total = jnp.zeros((VROWS, BROWS), F32)
            for b in range(NBIN):
                total = total + jnp.where(slot[b] == k, 1.0, 0.0) * pay[b]
            PAY[k] = total
        for j in range(1, sectors):
            pay_of(j).start()
        mine = pl.ds(az * CAP, CAP)
        GOT[mine] = PAY[mine]

    @pl.loop(0, SUBSTEPS)
    def _(s):
        droplets(s, 0)
        droplets(s, 1)

        @pl.when(s == SUBSTEPS - 1)
        def _():
            send_bins()

        copies = axial_of(s)
        axial_wait_send(copies)
        for p in range(2):
            for copy in azim_of(s, p):
                copy.wait_send()
        axial_wait_recv(copies)
        stencil(s, 0)

        @pl.when(s < SUBSTEPS - 1)
        def _():
            axial_start(axial_of(s + 1))
            for copy in azim_of(s + 1, 0):
                copy.start()

        @pl.when(s == SUBSTEPS - 1)
        def _():
            for a in (0, CA - 1):
                save(a).start()

        stencil(s, 1)

        @pl.when(s < SUBSTEPS - 1)
        def _():
            for copy in azim_of(s + 1, 1):
                copy.start()

    for a in range(1, CA - 1):
        save(a).start()
    for q in range(2):
        dep_of(SUBSTEPS - 1, q).wait_send()
    for j in range(1, sectors):
        pay_of(j).wait()
    moved_out[...] = GOT[...]
    for a in range(CA):
        save(a).wait()


def body(gas, diffusivity, swirl, drops, mass, azim_weight, cell_index, bin_rows, destination):
    sectors, slabs = lax.axis_size("azim"), lax.axis_size("axial")
    anywhere = pl.BlockSpec(memory_space=pl.ANY)
    vmem = pl.BlockSpec(memory_space=pltpu.VMEM)
    smem = pl.BlockSpec(memory_space=pltpu.SMEM)
    sem = pltpu.SemaphoreType.DMA
    gas_out, moved = pl.pallas_call(
        functools.partial(kernel, sectors, slabs),
        out_shape=(
            jax.ShapeDtypeStruct((NV, CA, CT, CR), F32),
            jax.ShapeDtypeStruct((sectors * CAP, VROWS, BROWS), F32),
        ),
        in_specs=[anywhere, smem, vmem, vmem, vmem, vmem, vmem, smem, smem],
        out_specs=(anywhere, vmem),
        scratch_shapes=[
            pltpu.VMEM((2, NV, CT, LANES), F32),
            pltpu.VMEM((ROWS, LANES), BF16),
            pltpu.VMEM((LANES, DROPLETS), BF16),
            pltpu.VMEM((DROPLETS, LANES), BF16),
            pltpu.VMEM((40, DROPLETS), F32),
            pltpu.VMEM((ROWS, DROPLETS), BF16),
            pltpu.VMEM((VROWS, DROPLETS), F32),
            pltpu.VMEM((8, DROPLETS), F32),
            pltpu.VMEM((VROWS, DROPLETS), F32),
            pltpu.VMEM((VROWS, DROPLETS), F32),
            pltpu.VMEM((MAIN + VROWS, LANES), F32),
            pltpu.VMEM((SUBSTEPS, 2, NV, CT, CR), F32),
            pltpu.VMEM((SUBSTEPS, VROWS, LANES), F32),
            pltpu.VMEM((SUBSTEPS, VROWS, LANES), F32),
            pltpu.VMEM((SUBSTEPS, VROWS, LANES), F32),
            pltpu.VMEM((VROWS, LANES), F32),
            pltpu.VMEM((VROWS, LANES), F32),
            pltpu.VMEM((sectors * CAP, VROWS, BROWS), F32),
            pltpu.VMEM((sectors * CAP, VROWS, BROWS), F32),
            sem((CA,)), sem((CA,)),
            sem((SUBSTEPS, 2)), sem((SUBSTEPS, 2)),
            sem((SUBSTEPS, 2)), sem((SUBSTEPS, 2)),
            sem((SUBSTEPS, 2)), sem((SUBSTEPS, 2)),
            sem((SUBSTEPS, 2)), sem((SUBSTEPS, 2)),
            sem((sectors,)), sem((sectors,)),
        ],
        compiler_params=pltpu.CompilerParams(
            collective_id=0, has_side_effects=True, vmem_limit_bytes=48 << 20
        ),
    )(gas, diffusivity, swirl, drops, mass, azim_weight, cell_index, bin_rows, destination)
    return gas_out, moved[:, :NV], moved[:, NV, 0].astype(jnp.int32)


def solution(mesh):
    return jax.shard_map(
        body,
        mesh=mesh,
        in_specs=(
            P(None, "axial", "azim", None),
            P(),
            P("axial", "azim", None),
            P(("axial", "azim"), None, None),
            P(("axial", "azim"), None),
            P(("axial", "azim"), None),
            P(("axial", "azim"), None),
            P(("axial", "azim")),
            P(("axial", "azim"), None),
        ),
        out_specs=(
            P(None, "axial", "azim", None),
            P(("axial", "azim"), None, None),
            P(("axial", "azim")),
        ),
        check_vma=False,
    )
```

time: 572 us -> 92.1 us (0.16); the launches traced: 561 us -> 91.8 us
  local copies, waits for them, and re-layouts: 270 us -> 9.36 us
  other arithmetic: 191 us -> 1.18 us
  Pallas kernels: 0 us -> 80.6 us
  starting transfers between devices: 50.5 us -> 0 us
  blocking collectives: 31.1 us -> 0 us
  between operations: 16.3 us -> 0.65 us
    scatter-add x8 -> x0, other arithmetic: 166 us -> none  [body(): jnp.zeros_like(field).at[:, first].add(part_low).at[:, second]]
    gather x16 -> x0, local copies, waits for them, and re-layouts: 105 us -> none  [the longest x8 54.2 us: body(): lower = jnp.take(field, first, axis=1)]
    pallas_call x0 -> x1, Pallas kernels: none -> 80.6 us  [body(): pl.pallas_call(functools.partial(kernel, sectors, slabs), out_shape=(jax....]
    slice x16 -> x0, local copies, waits for them, and re-layouts: 56.7 us -> none  [the longest x4 46.7 us: body(): inner = deposit[:, :, 1:cells_t + 1, :]]
    ppermute x20 -> x0, starting transfers between devices: 50.5 us -> none  [the longest x8 28.5 us: extended(): before = lax.ppermute(last, axis, up)]
    unnamed x154 -> x18, local copies, waits for them, and re-layouts: 50.9 us -> 9.36 us
    concatenate x4 -> x0, local copies, waits for them, and re-layouts: 40.1 us -> none  [extended(): shard = jnp.concatenate([before, shard, after], axis=dim)]
    unnamed x1 -> x0, blocking collectives: 31.1 us -> none
  transfers between devices with their start and end apart: 21 -> 0, of which waited for: 1 -> 0; matrix products, arithmetic and copies ran while one was open for 70% -> 0% of each run, Pallas kernels for 0% -> 0%
where the time goes in v1:
time: 92.1 us; the launch traced here: 91.8 us
  Pallas kernels  80.6 us (88%)
  local copies, waits for them, and re-layouts  9.36 us (10%)
  other arithmetic  1.18 us (1%)
    pallas_call x1, Pallas kernels, body(): pl.pallas_call(functools.partial(kernel, sectors, slabs), out_shape=(jax....  80.6 us
    unnamed x18, local copies, waits for them, and re-layouts  9.36 us

profile of v1, /device:TPU:0, one launch (start us, length us, event | category | flops | bytes accessed | tf_op | source)
XLA Modules:
  0.0 91.8 jit_solution(15865905928966261855)
XLA Ops:
  0.6 0.9 %copy.15.drops = f32[16,13,128]{2,1,0:T(8,128)S(1)} copy(f32[16,13,128]{2,0,1:T(8,128)} %param.12) | data formatting | bytes 212992 | tf_op args[3]
  1.6 0.7 copy.16.destination
  2.3 0.0 copy-start
  2.3 1.5 %copy-done = f32[13,8,32,128]{3,2,1,0:T(8,128)S(1)} copy-done((f32[13,8,32,128]{3,2,1,0:T(8,128)S(1)}, f32[13,8,32,128]{3,2,1,0:T(8,128)}, u32[]{:S(2)}) %copy-start) | copy-done | bytes 1703960
  3.8 0.0 copy-start.1
  3.8 0.9 copy-done.1
  4.7 0.0 copy-start.2
  4.7 0.7 copy-done.2
  5.4 0.0 copy-start.3
  5.4 0.7 copy-done.3
  6.1 0.0 copy-start.4
  6.1 0.7 copy-done.4
  6.8 0.0 copy-start.5
  6.8 0.7 copy-done.5
  7.4 0.0 copy-start.6
  7.4 0.7 copy-done.6
  8.1 80.6 %shard_map.112 = (f32[13,8,32,128]{3,2,1,0:T(8,128)S(1)}, f32[32,16,128]{2,1,0:T(8,128)S(1)}) custom-call(f32[13,8,32,128]{3,2,1,0:T(8,128)S(1)} %copy-done, f32[13]{0:T(128)S(1)} %copy-done.5, f32[8,32,128]{2,1,0:T(8,128)S(1)} %copy-done.1, f32[16,13,128]{2,1,0:T(8,128)S(1)} %copy.15.drops, f32[16,128]{1,0:T(8,128)S(1)} %copy-done.2, ...), custom_call_target="tpu_custom_call" | custom-call | tf_op jit(solution)/shard_map/pallas_call | solution.py:353
  88.7 0.8 copy.17
  89.4 1.2 %convert_reduce_fusion = s32[32]{0:T(128)} fusion(f32[32,16,128]{2,1,0:T(8,128)S(1)} %get-tuple-element.6), kind=kLoop, calls=%fused_computation | loop fusion | flops 32 | bytes 256 | tf_op jit(solution)/shard_map/convert_element_type | solution.py:392
  90.6 1.2 %copy.19 = f32[13,8,32,128]{3,2,1,0:T(8,128)} copy(f32[13,8,32,128]{3,2,1,0:T(8,128)S(1)} %get-tuple-element.16) | data formatting | bytes 3407872
Async XLA Ops:
  2.3 1.5 %copy-start = (f32[13,8,32,128]{3,2,1,0:T(8,128)S(1)}, f32[13,8,32,128]{3,2,1,0:T(8,128)}, u32[]{:S(2)}) copy-start(f32[13,8,32,128]{3,2,1,0:T(8,128)} %gas.1) | copy-start | bytes 5111812
  3.8 0.9 copy-start.1
  4.7 0.7 copy-start.2
  5.4 0.7 copy-start.3
  6.1 0.7 copy-start.4
  6.8 0.7 copy-start.5
  7.4 0.7 copy-start.6

commit v2 on v1

v2 whole, which is shorter than its diff:
```python
import functools

import jax
import jax.numpy as jnp
from jax import lax
from jax.experimental import pallas as pl
from jax.experimental.pallas import tpu as pltpu
from jax.sharding import PartitionSpec as P

MESH = pl.DeviceIdType.MESH
F32, BF16 = jnp.float32, jnp.bfloat16

SUBSTEPS = 4
CAP = 2
NV, CA, CT, CR = 13, 8, 32, 128
NBIN, BROWS = 16, 128
DROPLETS = NBIN * BROWS
LANES = CA * CR
MAIN = NV * CT
VROWS = 16
ROWS = 2 * MAIN + 2 * VROWS
HALF = CT // 2
CHUNK = 256

ORDER = (1, 2, 3, 4, 5, 6, 0, 7)
PLACE = {a: i for i, a in enumerate(ORDER)}
PARTS = ((768, 256, (0, 7)), (0, 512, (1, 2, 3, 4)), (512, 256, (5, 6)))
GROUPS = ((0, 5), (5, 4), (9, 4))


def lanes_of(a):
    return pl.ds(PLACE[a] * CR, CR)


def split(x):
    hi = x.astype(BF16)
    return hi, (x - hi.astype(F32)).astype(BF16)


def kernel(
    sectors, slabs,
    gas, diffusivity, swirl, drops, mass, azim_weight, cell_index, bin_rows, destination,
    gas_out, moved_out, rows_out,
    G, F, S, R, WHERE, W, L, D, Q, T, OUT, DEP, AX, LOW, HIGH, DEPR, FIRST, LAST, PAY, GOT, BINS, SW, MASS, WEIGHT, CELL, DROPS, FROM,
    small_sem, save_sem, ax_send, ax_recv, low_send, low_recv, high_send, high_recv, dep_send, dep_recv,
    pay_send, pay_recv,
):
    ax, az = lax.axis_index("axial"), lax.axis_index("azim")
    up_az, down_az = lax.rem(az + 1, sectors), lax.rem(az + sectors - 1, sectors)
    up_ax, down_ax = lax.rem(ax + 1, slabs), lax.rem(ax + slabs - 1, slabs)
    has_up, has_down = ax < slabs - 1, ax > 0

    small = [
        pltpu.make_async_copy(src, dst, small_sem.at[i])
        for i, (src, dst) in enumerate(
            ((mass, MASS), (azim_weight, WEIGHT), (cell_index, CELL), (drops, DROPS), (swirl, SW), (gas, G.at[0]))
        )
    ]

    def axial_of(s, g, layer):
        v0, count = GROUPS[g]
        vs = pl.ds(v0, count)
        upward = pltpu.make_async_remote_copy(
            layer(vs, CA - 1), AX.at[s, 0, vs], ax_send.at[s, 0, g], ax_recv.at[s, 0, g],
            device_id=(up_ax, az), device_id_type=MESH,
        )
        downward = pltpu.make_async_remote_copy(
            layer(vs, 0), AX.at[s, 1, vs], ax_send.at[s, 1, g], ax_recv.at[s, 1, g],
            device_id=(down_ax, az), device_id_type=MESH,
        )
        return upward, downward

    def both(first, first_do, second, second_do):
        @pl.when(first)
        def _():
            first_do()

        @pl.when(second)
        def _():
            second_do()

    def azim_of(s, p):
        lanes = pl.ds(*PARTS[p][:2])
        low = pltpu.make_async_remote_copy(
            LAST.at[:, lanes], LOW.at[s, :, lanes], low_send.at[s, p], low_recv.at[s, p],
            device_id=(ax, up_az), device_id_type=MESH,
        )
        high = pltpu.make_async_remote_copy(
            FIRST.at[:, lanes], HIGH.at[s, :, lanes], high_send.at[s, p], high_recv.at[s, p],
            device_id=(ax, down_az), device_id_type=MESH,
        )
        return low, high

    def dep_of(s, p):
        lanes = pl.ds(*PARTS[p][:2])
        return pltpu.make_async_remote_copy(
            DEP.at[pl.ds(MAIN, VROWS), lanes], DEPR.at[s, :, lanes], dep_send.at[s, p], dep_recv.at[s, p],
            device_id=(ax, up_az), device_id_type=MESH,
        )

    def pay_of(j):
        there = lax.rem(az + j, sectors)
        return pltpu.make_async_remote_copy(
            PAY.at[pl.ds(there * CAP, CAP)], GOT.at[pl.ds(az * CAP, CAP)], pay_send.at[j], pay_recv.at[j],
            device_id=(ax, there), device_id_type=MESH,
        )

    for copy in small:
        copy.start()
    D[...] = jnp.zeros((VROWS, DROPLETS), F32)
    barrier = pltpu.get_barrier_semaphore()
    for j in range(1, sectors):
        pl.semaphore_signal(
            barrier, inc=1, device_id=(ax, lax.rem(az + j, sectors)), device_id_type=MESH
        )
    for other in (up_ax, down_ax):
        pl.semaphore_signal(barrier, inc=1, device_id=(other, az), device_id_type=MESH)

    @pl.when(jnp.logical_not(has_down))
    def _():
        AX[:, 0] = jnp.zeros((SUBSTEPS, NV, CT, CR), F32)

    @pl.when(jnp.logical_not(has_up))
    def _():
        AX[:, 1] = jnp.zeros((SUBSTEPS, NV, CT, CR), F32)

    FIRST[...] = jnp.zeros((VROWS, LANES), F32)
    LAST[...] = jnp.zeros((VROWS, LANES), F32)
    T[...] = jnp.zeros((VROWS, DROPLETS), F32)
    BINS[0] = jnp.zeros((VROWS, BROWS), F32)
    slot = []
    for b in range(NBIN):
        rank = jnp.int32(0)
        for e in range(b):
            rank = rank + jnp.where(destination[e] == destination[b], 1, 0)
        slot.append(destination[b] * CAP + rank)
    for k in range(sectors * CAP):
        source = jnp.int32(0)
        for b in range(NBIN):
            source = source + jnp.where(slot[b] == k, b + 1, 0)
        FROM[k] = source

    for copy in small[:4]:
        copy.wait()
    cell = CELL[...]
    layer = cell // (CT * CR)
    place = jnp.where(layer == 0, CA - 2, jnp.where(layer == CA - 1, CA - 1, layer - 1))
    key = place * CR + cell % CR
    key_row = jnp.concatenate([key[b : b + 1] for b in range(NBIN)], axis=1)
    cell_row = jnp.concatenate([cell[b : b + 1] for b in range(NBIN)], axis=1)
    weight = jnp.concatenate([WEIGHT[b : b + 1, :] for b in range(NBIN)], axis=1)
    m = MASS[...]
    lane = lax.broadcasted_iota(jnp.int32, (1, BROWS), 1)
    half = 0.5 * m / (1.0 + m)
    live = [(lane < bin_rows[b]).astype(F32) for b in range(NBIN)]
    Q[0:1, :] = jnp.concatenate([half[b : b + 1] * live[b] for b in range(NBIN)], axis=1)
    for q in range(2):
        first, count, _ = PARTS[q]
        Q[q + 1 : q + 2, :] = jnp.where(
            key_row >= first, jnp.where(key_row < first + count, 1.0, 0.0), 0.0
        )
    azim_row = cell_row // CR % CT
    WHERE[0:1, :] = cell_row % CR
    WHERE[1:2, :] = cell_row // (CT * CR)
    for t0 in range(0, 40, 8):
        t = lax.broadcasted_iota(jnp.int32, (8, DROPLETS), 0) + t0
        W[t0 : t0 + 8, :] = jnp.where(t == azim_row, 1.0 - weight, 0.0) + jnp.where(
            t == azim_row + 1, weight, 0.0
        )

    @pl.loop(0, LANES // 16)
    def _(k):
        for c in range(0, DROPLETS, 4 * CHUNK):
            rows = lax.broadcasted_iota(jnp.int32, (16, 4 * CHUNK), 0) + k * 16
            R[pl.ds(pl.multiple_of(k * 16, 16), 16), c : c + 4 * CHUNK] = jnp.where(
                rows == key_row[:, c : c + 4 * CHUNK], 1.0, 0.0
            ).astype(BF16)

    pl.semaphore_wait(barrier, sectors + 1)
    for g in range(len(GROUPS)):
        upward, downward = axial_of(0, g, lambda vs, a: gas.at[vs, a])
        both(has_up, upward.start, has_down, downward.start)
    for copy in small[4:]:
        copy.wait()
    for v in range(NV):
        for a in range(CA):
            FIRST[v : v + 1, lanes_of(a)] = G[0, v, a, 0:1, :]
            LAST[v : v + 1, lanes_of(a)] = G[0, v, a, CT - 1 : CT, :]
    for p in range(len(PARTS)):
        for copy in azim_of(0, p):
            copy.start()
    for v in range(NV):
        for a in range(CA):
            hi, lo = split(G[0, v, a])
            F[v * CT : (v + 1) * CT, lanes_of(a)] = hi
            F[MAIN + v * CT : MAIN + (v + 1) * CT, lanes_of(a)] = lo
    for v in range(NV):
        for b in range(NBIN):
            D[v : v + 1, b * BROWS : (b + 1) * BROWS] = DROPS[v, b : b + 1, :]

    def gather(p):
        lanes = pl.ds(*PARTS[p][:2])
        for c in range(0, DROPLETS, CHUNK):
            ps = pl.ds(c, CHUNK)
            x = jnp.dot(F[:, lanes], R[lanes, ps], preferred_element_type=F32)
            near = (x[:MAIN] + x[MAIN:]).reshape(NV, CT, CHUNK)
            S[p, 0:NV, ps] = jnp.sum(near * W[0:CT, ps][None], axis=1)

    def finish(s, p):
        start, width, layers = PARTS[p]
        azim_of(s, p)[1].wait_recv()
        for c in range(0, DROPLETS, CHUNK):
            ps = pl.ds(c, CHUNK)
            far = []
            for e in range(c, c + CHUNK, BROWS):
                es = pl.ds(e, BROWS)
                at = jnp.broadcast_to(WHERE[0:1, es], (8, BROWS))
                tops = []
                for top in (0, 8):
                    total = jnp.zeros((8, BROWS), F32)
                    for a in layers:
                        value = jnp.take_along_axis(
                            HIGH[s, top : top + 8, lanes_of(a)], at, axis=1, mode="promise_in_bounds"
                        )
                        total = total + jnp.where(WHERE[1:2, es] == a, value, 0.0)
                    tops.append(total)
                far.append(jnp.concatenate(tops, axis=0))
            far = jnp.concatenate(far, axis=1)
            w, w_far = W[0:CT, ps], W[CT : CT + 1, ps]
            sample = S[p, 0:NV, ps] + w_far * far[0:NV]
            rate = Q[0:1, ps] * (1.0 + 0.5 * jnp.tanh(sample[0:1]))
            carried = D[0:NV, ps]
            transfer = rate * (carried - sample)
            if p == 0:
                OUT[0:NV, ps] = transfer
            elif p == 1:
                OUT[0:NV, ps] = jnp.where(Q[1:2, ps] > 0.0, OUT[0:NV, ps], transfer)
            else:
                D[0:NV, ps] = carried - jnp.where(
                    Q[1:2, ps] + Q[2:3, ps] > 0.0, OUT[0:NV, ps], transfer
                )
            twice = 2.0 * transfer
            T[0:NV, ps] = twice
            for v in range(NV):
                hi, lo = split(w * twice[v : v + 1])
                L[v * CT : (v + 1) * CT, ps] = hi
                L[MAIN + v * CT : MAIN + (v + 1) * CT, ps] = lo
            hi, lo = split(w_far * T[:, ps])
            L[2 * MAIN : 2 * MAIN + VROWS, ps] = hi
            L[2 * MAIN + VROWS : ROWS, ps] = lo

        if p == 0:
            @pl.when(s > 0)
            def _():
                for q in range(len(PARTS)):
                    dep_of(s - 1, q).wait_send()

        for k in range(start, start + width, CHUNK):
            ks = pl.ds(k, CHUNK)
            x = lax.dot_general(
                L[...], R[ks, :], (((1,), (1,)), ((), ())), preferred_element_type=F32
            )
            DEP[0:MAIN, ks] = x[:MAIN] + x[MAIN : 2 * MAIN]
            DEP[MAIN : MAIN + VROWS, ks] = x[2 * MAIN : 2 * MAIN + VROWS] + x[2 * MAIN + VROWS :]
        dep_of(s, p).start()

    def stencil(s, now, p, halves=(0, 1), vs=(0, NV)):
        later = 1 - now
        sub = lax.broadcasted_iota(jnp.int32, (8, CR), 0)
        column = lax.broadcasted_iota(jnp.int32, (8, CR), 1)
        for v in range(vs[0], vs[0] + vs[1]):
            d = diffusivity[v]
            own = 1.0 - 6.0 * d
            one = pl.ds(v, 1)
            for a in PARTS[p][2]:
                here = lanes_of(a)
                tiles = [G[now, v, a, i * 8 : i * 8 + 8] for i in range(CT // 8)]
                for half in halves:
                    out = []
                    for i in (2 * half, 2 * half + 1):
                        rows = pl.ds(i * 8, 8)
                        c = tiles[i]
                        first = LOW[s, one, here] if i == 0 else pltpu.roll(tiles[i - 1], 1, 0)
                        behind = jnp.where(sub == 0, first, pltpu.roll(c, 1, 0))
                        last = HIGH[s, one, here] if i == 3 else pltpu.roll(tiles[i + 1], 7, 0)
                        ahead = jnp.where(sub == 7, last, pltpu.roll(c, 7, 0))
                        below = AX[s, 0, v, rows] if a == 0 else G[now, v, a - 1, rows]
                        above = AX[s, 1, v, rows] if a == CA - 1 else G[now, v, a + 1, rows]
                        inward = jnp.where(column == 0, 0.0, pltpu.roll(c, 1, 1))
                        outward = jnp.where(column == CR - 1, 0.0, pltpu.roll(c, CR - 1, 1))
                        around = (behind + ahead) + (above + below) + (outward + inward)
                        new = (own * c + d * around) + (SW[a, rows] * (behind - c))
                        new = new + DEP[pl.ds(v * CT + i * 8, 8), here]
                        if i == 0:
                            new = new + jnp.where(sub == 0, DEPR[s, one, here], 0.0)
                            FIRST[one, here] = new[0:1]
                        if i == 3:
                            LAST[one, here] = new[7:8]
                        G[later, v, a, rows] = new
                        out.append(new)
                    hi, lo = split(jnp.concatenate(out, axis=0))
                    at = v * CT + half * 16
                    F[at : at + 16, here] = hi
                    F[MAIN + at : MAIN + at + 16, here] = lo

    def send_bins():
        row = lax.broadcasted_iota(jnp.int32, (VROWS, BROWS), 0)
        for b in range(NBIN):
            alive = (lane < bin_rows[b]).astype(F32)
            BINS[b + 1] = jnp.where(
                row == NV, bin_rows[b].astype(F32), D[:, b * BROWS : (b + 1) * BROWS] * alive
            )
        for k in range(sectors * CAP):
            PAY[k] = BINS[FROM[k]]
        for j in range(1, sectors):
            pay_of(j).start()
        mine = pl.ds(az * CAP, CAP)
        GOT[mine] = PAY[mine]

    def save(a):
        return pltpu.make_async_copy(G.at[SUBSTEPS % 2, :, a], gas_out.at[:, a], save_sem.at[a])

    gather(0)
    gather(1)

    def substep(s, now):
        further = s < SUBSTEPS - 1

        def when_further(do):
            if now == 0:
                do()
            else:
                pl.when(further)(do)

        finish(s, 0)
        finish(s, 1)
        gather(2)
        finish(s, 2)
        if now == 1:
            pl.when(jnp.logical_not(further))(send_bins)
        for p in range(len(PARTS)):
            low, high = azim_of(s, p)
            low.wait_send()
            high.wait_send()
            low.wait_recv()
        dep_of(s, 0).wait_recv()
        for g in range(len(GROUPS)):
            upward, downward = axial_of(s, g, lambda vs, a: G.at[now, vs, a])
            both(has_up, upward.wait_send, has_down, downward.wait_send)
            both(has_down, upward.wait_recv, has_up, downward.wait_recv)
            stencil(s, now, 0, vs=GROUPS[g])

            @when_further
            def _():
                upward, downward = axial_of(s + 1, g, lambda vs, a: G.at[1 - now, vs, a])
                both(has_up, upward.start, has_down, downward.start)

        @when_further
        def _():
            for copy in azim_of(s + 1, 0):
                copy.start()

        dep_of(s, 1).wait_recv()
        stencil(s, now, 1)

        @when_further
        def _():
            for copy in azim_of(s + 1, 1):
                copy.start()

        stencil(s, now, 2, (1,))

        @when_further
        def _():
            gather(0)
            gather(1)

        dep_of(s, 2).wait_recv()
        stencil(s, now, 2, (0,))

        @when_further
        def _():
            for copy in azim_of(s + 1, 2):
                copy.start()

    @pl.loop(0, SUBSTEPS // 2)
    def _(i):
        substep(2 * i, 0)
        substep(2 * i + 1, 1)

    for a in range(CA):
        save(a).start()
    for q in range(len(PARTS)):
        dep_of(SUBSTEPS - 1, q).wait_send()
    for j in range(1, sectors):
        pay_of(j).wait()
    lines = jnp.concatenate([GOT[k, NV : NV + 1, :] for k in range(sectors * CAP)], axis=0)
    at = lax.broadcasted_iota(jnp.int32, lines.shape, 0)
    column = lax.broadcasted_iota(jnp.int32, lines.shape, 1)
    counts = jnp.sum(jnp.where(at == column, lines, 0.0), axis=0)
    rows_out[...] = counts[: sectors * CAP].astype(jnp.int32)
    for k in range(sectors * CAP):
        for v in range(NV):
            moved_out[v, k : k + 1, :] = GOT[k, v : v + 1, :]
    for a in range(CA):
        save(a).wait()


def body(gas, diffusivity, swirl, drops, mass, azim_weight, cell_index, bin_rows, destination):
    sectors, slabs = lax.axis_size("azim"), lax.axis_size("axial")
    hbm = pl.BlockSpec(memory_space=pltpu.HBM)
    vmem = pl.BlockSpec(memory_space=pltpu.VMEM)
    smem = pl.BlockSpec(memory_space=pltpu.SMEM)
    sem = pltpu.SemaphoreType.DMA
    parts = len(PARTS)
    slots = sectors * CAP
    gas, moved, rows = pl.pallas_call(
        functools.partial(kernel, sectors, slabs),
        out_shape=(
            jax.ShapeDtypeStruct((NV, CA, CT, CR), F32),
            jax.ShapeDtypeStruct((NV, slots, BROWS), F32),
            jax.ShapeDtypeStruct((slots,), jnp.int32),
        ),
        in_specs=[hbm, smem, hbm, hbm, hbm, hbm, hbm, smem, smem],
        out_specs=(hbm, vmem, vmem),
        scratch_shapes=[
            pltpu.VMEM((2, NV, CA, CT, CR), F32),
            pltpu.VMEM((2 * MAIN, LANES), BF16),
            pltpu.VMEM((parts, VROWS, DROPLETS), F32),
            pltpu.VMEM((LANES, DROPLETS), BF16),
            pltpu.VMEM((8, DROPLETS), jnp.int32),
            pltpu.VMEM((40, DROPLETS), F32),
            pltpu.VMEM((ROWS, DROPLETS), BF16),
            pltpu.VMEM((VROWS, DROPLETS), F32),
            pltpu.VMEM((8, DROPLETS), F32),
            pltpu.VMEM((VROWS, DROPLETS), F32),
            pltpu.VMEM((VROWS, DROPLETS), F32),
            pltpu.VMEM((MAIN + VROWS, LANES), F32),
            pltpu.VMEM((SUBSTEPS, 2, NV, CT, CR), F32),
            pltpu.VMEM((SUBSTEPS, VROWS, LANES), F32),
            pltpu.VMEM((SUBSTEPS, VROWS, LANES), F32),
            pltpu.VMEM((SUBSTEPS, VROWS, LANES), F32),
            pltpu.VMEM((VROWS, LANES), F32),
            pltpu.VMEM((VROWS, LANES), F32),
            pltpu.VMEM((slots, VROWS, BROWS), F32),
            pltpu.VMEM((slots, VROWS, BROWS), F32),
            pltpu.VMEM((NBIN + 1, VROWS, BROWS), F32),
            pltpu.VMEM((CA, CT, CR), F32),
            pltpu.VMEM((NBIN, BROWS), F32),
            pltpu.VMEM((NBIN, BROWS), F32),
            pltpu.VMEM((NBIN, BROWS), jnp.int32),
            pltpu.VMEM((NV, NBIN, BROWS), F32),
            pltpu.SMEM((slots,), jnp.int32),
            sem((6,)), sem((CA,)),
            sem((SUBSTEPS, 2, len(GROUPS))), sem((SUBSTEPS, 2, len(GROUPS))),
            sem((SUBSTEPS, parts)), sem((SUBSTEPS, parts)),
            sem((SUBSTEPS, parts)), sem((SUBSTEPS, parts)),
            sem((SUBSTEPS, parts)), sem((SUBSTEPS, parts)),
            sem((sectors,)), sem((sectors,)),
        ],
        compiler_params=pltpu.CompilerParams(
            collective_id=0, has_side_effects=True, vmem_limit_bytes=62 << 20
        ),
    )(
        gas, diffusivity, swirl, jnp.swapaxes(drops, 0, 1), mass, azim_weight, cell_index, bin_rows,
        destination[:, 0],
    )
    return gas, jnp.swapaxes(moved, 0, 1), rows


def solution(mesh):
    return jax.shard_map(
        body,
        mesh=mesh,
        in_specs=(
            P(None, "axial", "azim", None),
            P(),
            P("axial", "azim", None),
            P(("axial", "azim"), None, None),
            P(("axial", "azim"), None),
            P(("axial", "azim"), None),
            P(("axial", "azim"), None),
            P(("axial", "azim")),
            P(("axial", "azim"), None),
        ),
        out_specs=(
            P(None, "axial", "azim", None),
            P(("axial", "azim"), None, None),
            P(("axial", "azim")),
        ),
        check_vma=False,
    )
```

time: 92.1 us -> 79.7 us (0.87); the launches traced: 91.8 us -> 78.5 us
  Pallas kernels: 80.6 us -> 73.8 us
  local copies, waits for them, and re-layouts: 9.36 us -> 4.02 us
  other arithmetic: 1.18 us -> 0 us
    pallas_call x1, Pallas kernels: 80.6 us -> 73.8 us  [body(): pl.pallas_call(functools.partial(kernel, sectors, slabs), out_shape=(jax....]
    unnamed x18 -> x7, local copies, waits for them, and re-layouts: 9.36 us -> 4.02 us
    convert_element_type x1 -> x0, other arithmetic: 1.18 us -> none  [body(): return (gas_out, moved[:, :NV], moved[:, NV, 0].astype(jnp.int32))]
where the time goes in v2:
time: 79.7 us; the launch traced here: 78.5 us
  Pallas kernels  73.8 us (93%)
  local copies, waits for them, and re-layouts  4.02 us (5%)
    pallas_call x1, Pallas kernels, body(): pl.pallas_call(functools.partial(kernel, sectors, slabs), out_shape=(jax....  73.8 us
    unnamed x7, local copies, waits for them, and re-layouts  4.02 us

profile of v2, /device:TPU:0, one launch (start us, length us, event | category | flops | bytes accessed | tf_op | source)
XLA Modules:
  0.0 78.5 jit_solution(7978741766528924548)
XLA Ops:
  0.6 73.8 %shard_map.112 = (f32[13,8,32,128]{3,2,1,0:T(8,128)}, f32[13,32,128]{2,1,0:T(8,128)}, s32[32]{0:T(128)}) custom-call(f32[13,8,32,128]{3,2,1,0:T(8,128)} %gas.1, f32[13]{0:T(128)} %diffusivity.1, f32[8,32,128]{2,1,0:T(8,128)} %swirl.1, f32[13,16,128]{2,1,0:T(8,128)} %bitcast.4, f32[16,128]{1,0:T(8,128)} %mass.1, f32[16,128]{1,0:T(8,128)} %azim_weight.1, ...), custom_call_target="tpu_custom_call" | custom-call | tf_op jit(solution)/shard_map/pallas_call | solution.py:417
  74.4 0.0 copy-start
  74.5 0.0 copy-start.1
  74.5 2.8 %copy.15 = f32[13,8,32,128]{3,2,1,0:T(8,128)} copy(f32[13,8,32,128]{3,2,1,0:T(8,128)} %get-tuple-element.12) | data formatting | bytes 3407872
  77.3 0.0 copy-done
  77.3 0.7 copy.16
  78.0 0.0 copy-done.1
  78.0 0.5 copy.17
Async XLA Ops:
  74.4 2.8 %copy-start = (f32[13,32,128]{2,1,0:T(8,128)S(1)}, f32[13,32,128]{2,1,0:T(8,128)}, u32[]{:S(2)}) copy-start(f32[13,32,128]{2,1,0:T(8,128)} %get-tuple-element.7) | copy-start | bytes 638980
  74.5 3.5 %copy-start.1 = (s32[32]{0:T(128)S(1)}, s32[32]{0:T(128)}, u32[]{:S(2)}) copy-start(s32[32]{0:T(128)} %get-tuple-element.14) | copy-start | bytes 388

commit v3 on v2

--- a/solution.py
+++ b/solution.py
@@ -198,18 +198,22 @@
         for b in range(NBIN):
             D[v : v + 1, b * BROWS : (b + 1) * BROWS] = DROPS[v, b : b + 1, :]
 
+    def gather_chunk(p, c):
+        lanes = pl.ds(*PARTS[p][:2])
+        ps = pl.ds(c, CHUNK)
+        x = jnp.dot(F[:, lanes], R[lanes, ps], preferred_element_type=F32)
+        near = (x[:MAIN] + x[MAIN:]).reshape(NV, CT, CHUNK)
+        S[p, 0:NV, ps] = jnp.sum(near * W[0:CT, ps][None], axis=1)
+
     def gather(p):
-        lanes = pl.ds(*PARTS[p][:2])
         for c in range(0, DROPLETS, CHUNK):
-            ps = pl.ds(c, CHUNK)
-            x = jnp.dot(F[:, lanes], R[lanes, ps], preferred_element_type=F32)
-            near = (x[:MAIN] + x[MAIN:]).reshape(NV, CT, CHUNK)
-            S[p, 0:NV, ps] = jnp.sum(near * W[0:CT, ps][None], axis=1)
-
-    def finish(s, p):
-        start, width, layers = PARTS[p]
-        azim_of(s, p)[1].wait_recv()
+            gather_chunk(p, c)
+
+    def transfers(s, p, beside=None):
+        layers = PARTS[p][2]
         for c in range(0, DROPLETS, CHUNK):
+            if beside is not None:
+                gather_chunk(beside, c)
             ps = pl.ds(c, CHUNK)
             far = []
             for e in range(c, c + CHUNK, BROWS):
@@ -243,26 +247,21 @@
             T[0:NV, ps] = twice
             for v in range(NV):
                 hi, lo = split(w * twice[v : v + 1])
-                L[v * CT : (v + 1) * CT, ps] = hi
-                L[MAIN + v * CT : MAIN + (v + 1) * CT, ps] = lo
+                L[p % 2, v * CT : (v + 1) * CT, ps] = hi
+                L[p % 2, MAIN + v * CT : MAIN + (v + 1) * CT, ps] = lo
             hi, lo = split(w_far * T[:, ps])
-            L[2 * MAIN : 2 * MAIN + VROWS, ps] = hi
-            L[2 * MAIN + VROWS : ROWS, ps] = lo
-
-        if p == 0:
-            @pl.when(s > 0)
-            def _():
-                for q in range(len(PARTS)):
-                    dep_of(s - 1, q).wait_send()
-
+            L[p % 2, 2 * MAIN : 2 * MAIN + VROWS, ps] = hi
+            L[p % 2, 2 * MAIN + VROWS : ROWS, ps] = lo
+
+    def deposit(s, p):
+        start, width, _ = PARTS[p]
         for k in range(start, start + width, CHUNK):
             ks = pl.ds(k, CHUNK)
             x = lax.dot_general(
-                L[...], R[ks, :], (((1,), (1,)), ((), ())), preferred_element_type=F32
+                L[p % 2], R[ks, :], (((1,), (1,)), ((), ())), preferred_element_type=F32
             )
             DEP[0:MAIN, ks] = x[:MAIN] + x[MAIN : 2 * MAIN]
             DEP[MAIN : MAIN + VROWS, ks] = x[2 * MAIN : 2 * MAIN + VROWS] + x[2 * MAIN + VROWS :]
-        dep_of(s, p).start()
 
     def stencil(s, now, p, halves=(0, 1), vs=(0, NV)):
         later = 1 - now
@@ -332,10 +331,18 @@
             else:
                 pl.when(further)(do)
 
-        finish(s, 0)
-        finish(s, 1)
-        gather(2)
-        finish(s, 2)
+        for p in range(2):
+            azim_of(s, p)[1].wait_recv()
+        transfers(s, 0, beside=2)
+        deposit(s, 0)
+        transfers(s, 1)
+        dep_of(s, 0).start()
+        deposit(s, 1)
+        dep_of(s, 1).start()
+        azim_of(s, 2)[1].wait_recv()
+        transfers(s, 2)
+        deposit(s, 2)
+        dep_of(s, 2).start()
         if now == 1:
             pl.when(jnp.logical_not(further))(send_bins)
         for p in range(len(PARTS)):
@@ -360,20 +367,31 @@
             for copy in azim_of(s + 1, 0):
                 copy.start()
 
+        def uppers():
+            stencil(s, now, 1, (1,))
+            stencil(s, now, 2, (1,))
+
+        @when_further
+        def _():
+            gather(0)
+            uppers()
+
+        if now == 1:
+            pl.when(jnp.logical_not(further))(uppers)
         dep_of(s, 1).wait_recv()
-        stencil(s, now, 1)
+        stencil(s, now, 1, (0,))
 
         @when_further
         def _():
             for copy in azim_of(s + 1, 1):
                 copy.start()
-
-        stencil(s, now, 2, (1,))
-
-        @when_further
-        def _():
-            gather(0)
             gather(1)
+
+        if now == 1:
+            @pl.when(jnp.logical_not(further))
+            def _():
+                for a in PARTS[0][2] + PARTS[1][2]:
+                    save(a).start()
 
         dep_of(s, 2).wait_recv()
         stencil(s, now, 2, (0,))
@@ -383,15 +401,16 @@
             for copy in azim_of(s + 1, 2):
                 copy.start()
 
+        for q in range(len(PARTS)):
+            dep_of(s, q).wait_send()
+
     @pl.loop(0, SUBSTEPS // 2)
     def _(i):
         substep(2 * i, 0)
         substep(2 * i + 1, 1)
 
-    for a in range(CA):
+    for a in PARTS[2][2]:
         save(a).start()
-    for q in range(len(PARTS)):
-        dep_of(SUBSTEPS - 1, q).wait_send()
     for j in range(1, sectors):
         pay_of(j).wait()
     lines = jnp.concatenate([GOT[k, NV : NV + 1, :] for k in range(sectors * CAP)], axis=0)
@@ -430,7 +449,7 @@
             pltpu.VMEM((LANES, DROPLETS), BF16),
             pltpu.VMEM((8, DROPLETS), jnp.int32),
             pltpu.VMEM((40, DROPLETS), F32),
-            pltpu.VMEM((ROWS, DROPLETS), BF16),
+            pltpu.VMEM((2, ROWS, DROPLETS), BF16),
             pltpu.VMEM((VROWS, DROPLETS), F32),
             pltpu.VMEM((8, DROPLETS), F32),
             pltpu.VMEM((VROWS, DROPLETS), F32),

time: 79.7 us -> 71.6 us (0.90)
  Pallas kernels: 73.8 us -> 65.8 us
    pallas_call x1, Pallas kernels: 73.8 us -> 65.8 us  [body(): pl.pallas_call(functools.partial(kernel, sectors, slabs), out_shape=(jax....]
where the time goes in v3:
time: 71.6 us; the launch traced here: 70.5 us
  Pallas kernels  65.8 us (92%)
  local copies, waits for them, and re-layouts  4.02 us (6%)
    pallas_call x1, Pallas kernels, body(): pl.pallas_call(functools.partial(kernel, sectors, slabs), out_shape=(jax....  65.8 us
    unnamed x7, local copies, waits for them, and re-layouts  4.02 us

profile of v3, /device:TPU:0, one launch (start us, length us, event | category | flops | bytes accessed | tf_op | source)
XLA Modules:
  0.0 70.5 jit_solution(2565332217543334041)
XLA Ops:
  0.6 65.8 %shard_map.112 = (f32[13,8,32,128]{3,2,1,0:T(8,128)}, f32[13,32,128]{2,1,0:T(8,128)}, s32[32]{0:T(128)}) custom-call(f32[13,8,32,128]{3,2,1,0:T(8,128)} %gas.1, f32[13]{0:T(128)} %diffusivity.1, f32[8,32,128]{2,1,0:T(8,128)} %swirl.1, f32[13,16,128]{2,1,0:T(8,128)} %bitcast.4, f32[16,128]{1,0:T(8,128)} %mass.1, f32[16,128]{1,0:T(8,128)} %azim_weight.1, ...), custom_call_target="tpu_custom_call" | custom-call | tf_op jit(solution)/shard_map/pallas_call | solution.py:436
  66.5 0.0 copy-start
  66.5 0.0 copy-start.1
  66.5 2.8 %copy.15 = f32[13,8,32,128]{3,2,1,0:T(8,128)} copy(f32[13,8,32,128]{3,2,1,0:T(8,128)} %get-tuple-element.12) | data formatting | bytes 3407872
  69.3 0.0 copy-done
  69.3 0.7 copy.16
  70.0 0.0 copy-done.1
  70.0 0.5 copy.17
Async XLA Ops:
  66.5 2.8 %copy-start = (f32[13,32,128]{2,1,0:T(8,128)S(1)}, f32[13,32,128]{2,1,0:T(8,128)}, u32[]{:S(2)}) copy-start(f32[13,32,128]{2,1,0:T(8,128)} %get-tuple-element.7) | copy-start | bytes 638980
  66.5 3.5 %copy-start.1 = (s32[32]{0:T(128)S(1)}, s32[32]{0:T(128)}, u32[]{:S(2)}) copy-start(s32[32]{0:T(128)} %get-tuple-element.14) | copy-start | bytes 388

commit v4 on v3

--- a/solution.py
+++ b/solution.py
@@ -48,7 +48,7 @@
     ax, az = lax.axis_index("axial"), lax.axis_index("azim")
     up_az, down_az = lax.rem(az + 1, sectors), lax.rem(az + sectors - 1, sectors)
     up_ax, down_ax = lax.rem(ax + 1, slabs), lax.rem(ax + slabs - 1, slabs)
-    has_up, has_down = ax < slabs - 1, ax > 0
+    low_on, high_on = jnp.where(ax > 0, 1.0, 0.0), jnp.where(ax < slabs - 1, 1.0, 0.0)
 
     small = [
         pltpu.make_async_copy(src, dst, small_sem.at[i])
@@ -69,15 +69,6 @@
             device_id=(down_ax, az), device_id_type=MESH,
         )
         return upward, downward
-
-    def both(first, first_do, second, second_do):
-        @pl.when(first)
-        def _():
-            first_do()
-
-        @pl.when(second)
-        def _():
-            second_do()
 
     def azim_of(s, p):
         lanes = pl.ds(*PARTS[p][:2])
@@ -115,14 +106,6 @@
         )
     for other in (up_ax, down_ax):
         pl.semaphore_signal(barrier, inc=1, device_id=(other, az), device_id_type=MESH)
-
-    @pl.when(jnp.logical_not(has_down))
-    def _():
-        AX[:, 0] = jnp.zeros((SUBSTEPS, NV, CT, CR), F32)
-
-    @pl.when(jnp.logical_not(has_up))
-    def _():
-        AX[:, 1] = jnp.zeros((SUBSTEPS, NV, CT, CR), F32)
 
     FIRST[...] = jnp.zeros((VROWS, LANES), F32)
     LAST[...] = jnp.zeros((VROWS, LANES), F32)
@@ -168,18 +151,19 @@
             t == azim_row + 1, weight, 0.0
         )
 
-    @pl.loop(0, LANES // 16)
-    def _(k):
+    def one_hot(k):
         for c in range(0, DROPLETS, 4 * CHUNK):
             rows = lax.broadcasted_iota(jnp.int32, (16, 4 * CHUNK), 0) + k * 16
             R[pl.ds(pl.multiple_of(k * 16, 16), 16), c : c + 4 * CHUNK] = jnp.where(
                 rows == key_row[:, c : c + 4 * CHUNK], 1.0, 0.0
             ).astype(BF16)
 
+    pl.loop(0, LANES // 32)(one_hot)
     pl.semaphore_wait(barrier, sectors + 1)
     for g in range(len(GROUPS)):
-        upward, downward = axial_of(0, g, lambda vs, a: gas.at[vs, a])
-        both(has_up, upward.start, has_down, downward.start)
+        for copy in axial_of(0, g, lambda vs, a: gas.at[vs, a]):
+            copy.start()
+    pl.loop(LANES // 32, LANES // 16)(one_hot)
     for copy in small[4:]:
         copy.wait()
     for v in range(NV):
@@ -283,8 +267,8 @@
                         behind = jnp.where(sub == 0, first, pltpu.roll(c, 1, 0))
                         last = HIGH[s, one, here] if i == 3 else pltpu.roll(tiles[i + 1], 7, 0)
                         ahead = jnp.where(sub == 7, last, pltpu.roll(c, 7, 0))
-                        below = AX[s, 0, v, rows] if a == 0 else G[now, v, a - 1, rows]
-                        above = AX[s, 1, v, rows] if a == CA - 1 else G[now, v, a + 1, rows]
+                        below = AX[s, 0, v, rows] * low_on if a == 0 else G[now, v, a - 1, rows]
+                        above = AX[s, 1, v, rows] * high_on if a == CA - 1 else G[now, v, a + 1, rows]
                         inward = jnp.where(column == 0, 0.0, pltpu.roll(c, 1, 1))
                         outward = jnp.where(column == CR - 1, 0.0, pltpu.roll(c, CR - 1, 1))
                         around = (behind + ahead) + (above + below) + (outward + inward)
@@ -352,15 +336,14 @@
             low.wait_recv()
         dep_of(s, 0).wait_recv()
         for g in range(len(GROUPS)):
-            upward, downward = axial_of(s, g, lambda vs, a: G.at[now, vs, a])
-            both(has_up, upward.wait_send, has_down, downward.wait_send)
-            both(has_down, upward.wait_recv, has_up, downward.wait_recv)
+            for copy in axial_of(s, g, lambda vs, a: G.at[now, vs, a]):
+                copy.wait()
             stencil(s, now, 0, vs=GROUPS[g])
 
             @when_further
             def _():
-                upward, downward = axial_of(s + 1, g, lambda vs, a: G.at[1 - now, vs, a])
-                both(has_up, upward.start, has_down, downward.start)
+                for copy in axial_of(s + 1, g, lambda vs, a: G.at[1 - now, vs, a]):
+                    copy.start()
 
         @when_further
         def _():

time: 71.6 us -> 71.2 us (level)
  no operation moved by 1% of the time
where the time goes in v4:
time: 71.2 us; the launch traced here: 70.6 us
  Pallas kernels  65.9 us (93%)
  local copies, waits for them, and re-layouts  4.02 us (6%)
    pallas_call x1, Pallas kernels, body(): pl.pallas_call(functools.partial(kernel, sectors, slabs), out_shape=(jax....  65.9 us
    unnamed x7, local copies, waits for them, and re-layouts  4.02 us

profile of v4, /device:TPU:0, one launch (start us, length us, event | category | flops | bytes accessed | tf_op | source)
XLA Modules:
  0.0 70.6 jit_solution(6903540955070674307)
XLA Ops:
  0.6 65.9 %shard_map.112 = (f32[13,8,32,128]{3,2,1,0:T(8,128)}, f32[13,32,128]{2,1,0:T(8,128)}, s32[32]{0:T(128)}) custom-call(f32[13,8,32,128]{3,2,1,0:T(8,128)} %gas.1, f32[13]{0:T(128)} %diffusivity.1, f32[8,32,128]{2,1,0:T(8,128)} %swirl.1, f32[13,16,128]{2,1,0:T(8,128)} %bitcast.4, f32[16,128]{1,0:T(8,128)} %mass.1, f32[16,128]{1,0:T(8,128)} %azim_weight.1, ...), custom_call_target="tpu_custom_call" | custom-call | tf_op jit(solution)/shard_map/pallas_call | solution.py:419
  66.5 0.0 copy-start
  66.5 0.0 copy-start.1
  66.6 2.8 %copy.15 = f32[13,8,32,128]{3,2,1,0:T(8,128)} copy(f32[13,8,32,128]{3,2,1,0:T(8,128)} %get-tuple-element.12) | data formatting | bytes 3407872
  69.4 0.0 copy-done
  69.4 0.7 copy.16
  70.1 0.0 copy-done.1
  70.1 0.5 copy.17
Async XLA Ops:
  66.5 2.8 %copy-start = (f32[13,32,128]{2,1,0:T(8,128)S(1)}, f32[13,32,128]{2,1,0:T(8,128)}, u32[]{:S(2)}) copy-start(f32[13,32,128]{2,1,0:T(8,128)} %get-tuple-element.7) | copy-start | bytes 638980
  66.5 3.5 %copy-start.1 = (s32[32]{0:T(128)S(1)}, s32[32]{0:T(128)}, u32[]{:S(2)}) copy-start(s32[32]{0:T(128)} %get-tuple-element.14) | copy-start | bytes 388
